TPU v7x, 128 devices: a whole 4x4x4 slice. The times are simulated.
128 devices in a mesh: dom: 16 (over x, z), sub: 8 (over y, core).
Axes of the slice: x: 4, y: 4, z: 4, core: 2. Of those that a mesh axis runs over, the one named last changes fastest.
Arguments:
- segments: float32 [16384, 9, 128], P(('dom', 'sub')), may hold values from -6 to 6
- send_tiles: int32 [128, 128, 4], P(('dom', 'sub')), may hold values from 0 to 127
- pair_local: int32 [128, 512], P(('dom', 'sub')), may hold values from 0 to 127
- pair_remote: int32 [128, 512], P(('dom', 'sub')), may hold values from 0 to 511, each once within a row
- pair_count: int32 [128], P(('dom', 'sub')), may hold values from 64 to 512, as said below
- tile_cell: int32 [16384], P(('dom', 'sub')), may hold values from 0 to 63
Outputs:
- forces: float32 [16384, 3, 128], P(('dom', 'sub'))
Inputs may be any that keep to these rules, and one draw needn't show every extreme that they name: `send_tiles`: every slot names a tile; each device sends exactly 4 tiles to every device. `pair_remote`: each device's row names every one of its 512 received slots once. `pair_count`: some device holds 512 live pairs.
All inputs are finite; a program needn't handle non-finite values.
Results may differ from a plain program's by a relative error of at most 0.00018.
Values sent between devices are 32-bit elements; how exact they have to be, the bound alone decides.
A program may use at most 64 MiB of HBM per device.

v0:
```python
import jax
import jax.numpy as jnp
from jax import lax
from jax.sharding import PartitionSpec as P

BLOCK = 64
NCELL = 64


core_square = 0.25


def interact(near_block, far_block, live_mask):
    apart = near_block[:, 0:3, :, None] - far_block[:, 0:3, None, :]
    spread = jnp.sum(apart * apart, axis=1) + core_square
    inverse = lax.rsqrt(spread)
    inverse = inverse * inverse * inverse
    burgers_dot = jnp.sum(near_block[:, 3:6, :, None] * far_block[:, 3:6, None, :], axis=1)
    cross_first = jnp.sum(near_block[:, 3:6, :, None] * far_block[:, 6:9, None, :], axis=1)
    cross_second = jnp.sum(far_block[:, 3:6, None, :] * near_block[:, 6:9, :, None], axis=1)
    coupling = (burgers_dot + cross_first * cross_second) * inverse * live_mask[:, None, None]
    weighted = apart * coupling[:, None]
    return (jnp.sum(weighted, axis=3), -jnp.sum(weighted, axis=2))


def far_field(segments, tile_cell, moment_sums, total_segments):
    moments = moment_sums.reshape(NCELL, 3, 3) / jnp.sqrt(jnp.float32(total_segments))
    moments = 0.5 * (moments + jnp.transpose(moments, (0, 2, 1)))
    cells = jnp.arange(NCELL).astype(jnp.float32)
    weights = 8.0 / (8.0 + jnp.abs(cells[:, None] - cells[None, :]))
    stress = jnp.dot(weights, moments.reshape(NCELL, 9), precision=lax.Precision.HIGHEST)
    onehot = (tile_cell[:, None] == jnp.arange(NCELL)[None, :]).astype(jnp.float32)
    tile_stress = jnp.dot(onehot, stress, precision=lax.Precision.HIGHEST).reshape(-1, 3, 3)
    traction = jnp.sum(tile_stress[:, :, :, None] * segments[:, None, 3:6, :], axis=2)
    lines = segments[:, 6:9, :]
    return jnp.stack(
        [
            traction[:, 1] * lines[:, 2] - traction[:, 2] * lines[:, 1],
            traction[:, 2] * lines[:, 0] - traction[:, 0] * lines[:, 2],
            traction[:, 0] * lines[:, 1] - traction[:, 1] * lines[:, 0],
        ],
        axis=1,
    )


def local_moments(segments, tile_cell):
    outer = jnp.sum(segments[:, 3:6, None, :] * segments[:, None, 6:9, :], axis=3).reshape(-1, 9)
    onehot = (jnp.arange(NCELL)[:, None] == tile_cell[None, :]).astype(jnp.float32)
    return jnp.dot(onehot, outer, precision=lax.Precision.HIGHEST)


def on_device(segments, send_tiles, pair_local, pair_remote, pair_count, tile_cell):
    width = segments.shape[2]
    peers = send_tiles.shape[1]
    slots = send_tiles.shape[2]
    n_dom = lax.axis_size("dom")
    n_sub = lax.axis_size("sub")
    outgoing = segments[send_tiles[0]]
    arrived = lax.all_to_all(outgoing, ("dom", "sub"), split_axis=0, concat_axis=0, tiled=True)
    arrived = arrived.reshape(peers * slots, 9, width)
    moment_sums = lax.psum(local_moments(segments, tile_cell), ("dom", "sub"))
    live_total = pair_count[0]
    local_blocks = pair_local[0].reshape(-1, BLOCK)
    remote_blocks = pair_remote[0].reshape(-1, BLOCK)
    block_numbers = jnp.arange(local_blocks.shape[0])

    def advance(carry, inputs):
        near_forces, far_forces = carry
        local_ids, remote_ids, block_number = inputs
        position = block_number * BLOCK + jnp.arange(BLOCK)
        live_mask = (position < live_total).astype(jnp.float32)
        near_part, far_part = interact(segments[local_ids], arrived[remote_ids], live_mask)
        return (
            (near_forces.at[local_ids].add(near_part), far_forces.at[remote_ids].add(far_part)),
            None,
        )

    start_near = jnp.zeros((segments.shape[0], 3, width), jnp.float32)
    start_far = jnp.zeros((peers * slots, 3, width), jnp.float32)
    totals, unused = lax.scan(
        advance, (start_near, start_far), (local_blocks, remote_blocks, block_numbers)
    )
    near_forces, far_forces = totals
    returned = lax.all_to_all(
        far_forces.reshape(peers, slots, 3, width),
        ("dom", "sub"),
        split_axis=0,
        concat_axis=0,
        tiled=True,
    )
    returned = returned.reshape(peers * slots, 3, width)
    pair_forces = near_forces.at[send_tiles[0].reshape(-1)].add(returned)
    total_segments = segments.shape[0] * width * n_dom * n_sub
    return pair_forces + far_field(segments, tile_cell, moment_sums, total_segments)


def solution(mesh):
    in_specs = (
        P(("dom", "sub"), None, None),
        P(("dom", "sub"), None, None),
        P(("dom", "sub"), None),
        P(("dom", "sub"), None),
        P(("dom", "sub")),
        P(("dom", "sub")),
    )
    out_specs = P(("dom", "sub"), None, None)
    return jax.shard_map(
        on_device, mesh=mesh, in_specs=in_specs, out_specs=out_specs, check_vma=False
    )
```

profile of v0, /device:TPU:1, one launch (start us, length us, event | category | flops | bytes accessed | tf_op | source)
XLA Modules:
  0.0 521.4 jit_solution(357893977652213291)
XLA Ops:
  0.9 4.6 gather_fusion.2
  7.4 11.9 %all-to-all-start = ((f32[128,4,9,128]{3,1,2,0:T(4,128)}), f32[128,4,9,128]{3,1,2,0:T(4,128)}, u32[]{:S(2)}, u32[]{:S(2)}) async-start(f32[128,4,9,128]{3,1,2,0:T(4,128)} %copy.64), calls=%async_computation | async-start | bytes 4718592 | tf_op jit(solution)/shard_map/all_to_all | solution.py:59
  20.2 83.5 %psum.7 = f32[64,9]{0,1:T(8,128)S(1)} all-reduce(f32[64,9]{0,1:T(8,128)S(1)} %fusion.10), channel_id=1, replica_groups=mesh['dom'=16,'sub'=8] {'dom','sub'}, use_global_device_ids=true, to_apply=%region_11.12 | all-reduce | flops 576 | bytes 4608 | tf_op jit(solution)/shard_map/psum | solution.py:61
  108.3 3.4 copy.67
  112.9 366.0 %while.12 = (s32[]{:T(128)}, f32[128,3,128]{2,1,0:T(4,128)S(1)}, f32[512,3,128]{2,1,0:T(4,128)}, s32[8,64]{1,0:T(8,128)S(1)}, f32[128,9,128]{2,1,0:T(8,128)S(1)}...) while((s32[]{:T(128)}, f32[128,3,128]{2,1,0:T(4,128)S(1)}, ...), condition=%wide.region_9.10_spmd, body=%wide.region_0.9_spmd.sunk | while | flops 44067392 | bytes 62860460 | solution.py:80
  113.7 2.8 gather_fusion
  116.6 13.1 %multiply_reduce_fusion.6 = (f32[64,128,128]{2,1,0:T(8,128)}, f32[64,128,128]{2,1,0:T(8,128)}, f32[64,128,128]{2,1,0:T(8,128)}) fusion(f32[64,3,128]{2,1,0:T(4,128)S(1)} %get-tuple-element.202, f32[64,3,128]{2,1,0:T(4,128)S(1)} %get-tuple-element.203, f32[64,3,128]{2,1,0:T(4,128)S(1)} %get-tuple-element.204, f32[64,3,128]{2,1,0:T(4,128)S(1)} %get-tuple-element.205), kind=kLoop, calls=%fused_computation.11.clone.1 | loop fusion | flops 15728640 | bytes 12976128 | tf_op jit(solution)/shard_map/while/body/eval_jaxpr/reduce_sum | solution.py:20
  129.6 4.1 fusion.33
  135.6 5.6 %fusion.34 = f32[64,128,128]{2,1,0:T(8,128)S(1)} fusion(f32[64,128,128]{2,1,0:T(8,128)S(1)} %fusion.33, f32[64,128,128]{2,1,0:T(8,128)} %get-tuple-element.206, f32[64,128,128]{2,1,0:T(8,128)} %get-tuple-element.207, f32[64,128,128]{2,1,0:T(8,128)S(1)} %copy-done.1, f32[64]{0:T(128)S(1)} %compare_convert_fusion.2), kind=kLoop, calls=%fused_computation.16.clone.1 | loop fusion | flops 7340032 | bytes 20971776 | tf_op jit(solution)/shard_map/while/body/eval_jaxpr/mul | solution.py:21
  141.2 8.0 %fusion.35 = (f32[64,3,128]{2,1,0:T(4,128)S(1)}, f32[64,3,128]{2,1,0:T(4,128)S(1)}) fusion(f32[64,128,128]{2,1,0:T(8,128)S(1)} %fusion.34, f32[64,3,128]{2,1,0:T(4,128)S(1)} %get-tuple-element.200, f32[64,3,128]{2,1,0:T(4,128)S(1)} %get-tuple-element.201), kind=kLoop, calls=%fused_computation.8.clone.1 | loop fusion | flops 12533760 | bytes 4587520 | tf_op jit(solution)/shard_map/while/body/eval_jaxpr/reduce_sum | solution.py:23
  149.2 6.7 %scatter_fusion.1 = f32[512,3,128]{2,1,0:T(4,128)} fusion(f32[512,3,128]{2,1,0:T(4,128)} %get-tuple-element.224, s32[64]{0:T(128)S(1)} %get-tuple-element.199, f32[64,3,128]{2,1,0:T(4,128)S(1)} %neg.4), kind=kCustom, calls=%fused_computation.4.clone.1 | custom fusion | flops 24576 | bytes 295168 | tf_op jit(solution)/shard_map/while/body/eval_jaxpr/scatter-add | solution.py:74
  155.9 2.7 scatter_fusion
  159.4 2.8 gather_fusion
  162.3 13.1 %multiply_reduce_fusion.6 = (f32[64,128,128]{2,1,0:T(8,128)}, f32[64,128,128]{2,1,0:T(8,128)}, f32[64,128,128]{2,1,0:T(8,128)}) fusion(f32[64,3,128]{2,1,0:T(4,128)S(1)} %get-tuple-element.202, f32[64,3,128]{2,1,0:T(4,128)S(1)} %get-tuple-element.203, f32[64,3,128]{2,1,0:T(4,128)S(1)} %get-tuple-element.204, f32[64,3,128]{2,1,0:T(4,128)S(1)} %get-tuple-element.205), kind=kLoop, calls=%fused_computation.11.clone.1 | loop fusion | flops 15728640 | bytes 12976128 | tf_op jit(solution)/shard_map/while/body/eval_jaxpr/reduce_sum | solution.py:20
  175.4 4.1 fusion.33
  181.3 5.6 %fusion.34 = f32[64,128,128]{2,1,0:T(8,128)S(1)} fusion(f32[64,128,128]{2,1,0:T(8,128)S(1)} %fusion.33, f32[64,128,128]{2,1,0:T(8,128)} %get-tuple-element.206, f32[64,128,128]{2,1,0:T(8,128)} %get-tuple-element.207, f32[64,128,128]{2,1,0:T(8,128)S(1)} %copy-done.1, f32[64]{0:T(128)S(1)} %compare_convert_fusion.2), kind=kLoop, calls=%fused_computation.16.clone.1 | loop fusion | flops 7340032 | bytes 20971776 | tf_op jit(solution)/shard_map/while/body/eval_jaxpr/mul | solution.py:21
  186.9 8.0 %fusion.35 = (f32[64,3,128]{2,1,0:T(4,128)S(1)}, f32[64,3,128]{2,1,0:T(4,128)S(1)}) fusion(f32[64,128,128]{2,1,0:T(8,128)S(1)} %fusion.34, f32[64,3,128]{2,1,0:T(4,128)S(1)} %get-tuple-element.200, f32[64,3,128]{2,1,0:T(4,128)S(1)} %get-tuple-element.201), kind=kLoop, calls=%fused_computation.8.clone.1 | loop fusion | flops 12533760 | bytes 4587520 | tf_op jit(solution)/shard_map/while/body/eval_jaxpr/reduce_sum | solution.py:23
  194.9 6.7 %scatter_fusion.1 = f32[512,3,128]{2,1,0:T(4,128)} fusion(f32[512,3,128]{2,1,0:T(4,128)} %get-tuple-element.224, s32[64]{0:T(128)S(1)} %get-tuple-element.199, f32[64,3,128]{2,1,0:T(4,128)S(1)} %neg.4), kind=kCustom, calls=%fused_computation.4.clone.1 | custom fusion | flops 24576 | bytes 295168 | tf_op jit(solution)/shard_map/while/body/eval_jaxpr/scatter-add | solution.py:74
  201.7 2.7 scatter_fusion
  205.2 2.8 gather_fusion
  208.1 13.1 %multiply_reduce_fusion.6 = (f32[64,128,128]{2,1,0:T(8,128)}, f32[64,128,128]{2,1,0:T(8,128)}, f32[64,128,128]{2,1,0:T(8,128)}) fusion(f32[64,3,128]{2,1,0:T(4,128)S(1)} %get-tuple-element.202, f32[64,3,128]{2,1,0:T(4,128)S(1)} %get-tuple-element.203, f32[64,3,128]{2,1,0:T(4,128)S(1)} %get-tuple-element.204, f32[64,3,128]{2,1,0:T(4,128)S(1)} %get-tuple-element.205), kind=kLoop, calls=%fused_computation.11.clone.1 | loop fusion | flops 15728640 | bytes 12976128 | tf_op jit(solution)/shard_map/while/body/eval_jaxpr/reduce_sum | solution.py:20
  221.1 4.1 fusion.33
  227.1 5.6 %fusion.34 = f32[64,128,128]{2,1,0:T(8,128)S(1)} fusion(f32[64,128,128]{2,1,0:T(8,128)S(1)} %fusion.33, f32[64,128,128]{2,1,0:T(8,128)} %get-tuple-element.206, f32[64,128,128]{2,1,0:T(8,128)} %get-tuple-element.207, f32[64,128,128]{2,1,0:T(8,128)S(1)} %copy-done.1, f32[64]{0:T(128)S(1)} %compare_convert_fusion.2), kind=kLoop, calls=%fused_computation.16.clone.1 | loop fusion | flops 7340032 | bytes 20971776 | tf_op jit(solution)/shard_map/while/body/eval_jaxpr/mul | solution.py:21
  232.7 8.0 %fusion.35 = (f32[64,3,128]{2,1,0:T(4,128)S(1)}, f32[64,3,128]{2,1,0:T(4,128)S(1)}) fusion(f32[64,128,128]{2,1,0:T(8,128)S(1)} %fusion.34, f32[64,3,128]{2,1,0:T(4,128)S(1)} %get-tuple-element.200, f32[64,3,128]{2,1,0:T(4,128)S(1)} %get-tuple-element.201), kind=kLoop, calls=%fused_computation.8.clone.1 | loop fusion | flops 12533760 | bytes 4587520 | tf_op jit(solution)/shard_map/while/body/eval_jaxpr/reduce_sum | solution.py:23
  240.7 6.7 %scatter_fusion.1 = f32[512,3,128]{2,1,0:T(4,128)} fusion(f32[512,3,128]{2,1,0:T(4,128)} %get-tuple-element.224, s32[64]{0:T(128)S(1)} %get-tuple-element.199, f32[64,3,128]{2,1,0:T(4,128)S(1)} %neg.4), kind=kCustom, calls=%fused_computation.4.clone.1 | custom fusion | flops 24576 | bytes 295168 | tf_op jit(solution)/shard_map/while/body/eval_jaxpr/scatter-add | solution.py:74
  247.4 2.7 scatter_fusion
  250.9 2.8 gather_fusion
  253.8 13.1 %multiply_reduce_fusion.6 = (f32[64,128,128]{2,1,0:T(8,128)}, f32[64,128,128]{2,1,0:T(8,128)}, f32[64,128,128]{2,1,0:T(8,128)}) fusion(f32[64,3,128]{2,1,0:T(4,128)S(1)} %get-tuple-element.202, f32[64,3,128]{2,1,0:T(4,128)S(1)} %get-tuple-element.203, f32[64,3,128]{2,1,0:T(4,128)S(1)} %get-tuple-element.204, f32[64,3,128]{2,1,0:T(4,128)S(1)} %get-tuple-element.205), kind=kLoop, calls=%fused_computation.11.clone.1 | loop fusion | flops 15728640 | bytes 12976128 | tf_op jit(solution)/shard_map/while/body/eval_jaxpr/reduce_sum | solution.py:20
  266.8 4.1 fusion.33
  272.8 5.6 %fusion.34 = f32[64,128,128]{2,1,0:T(8,128)S(1)} fusion(f32[64,128,128]{2,1,0:T(8,128)S(1)} %fusion.33, f32[64,128,128]{2,1,0:T(8,128)} %get-tuple-element.206, f32[64,128,128]{2,1,0:T(8,128)} %get-tuple-element.207, f32[64,128,128]{2,1,0:T(8,128)S(1)} %copy-done.1, f32[64]{0:T(128)S(1)} %compare_convert_fusion.2), kind=kLoop, calls=%fused_computation.16.clone.1 | loop fusion | flops 7340032 | bytes 20971776 | tf_op jit(solution)/shard_map/while/body/eval_jaxpr/mul | solution.py:21
  278.4 8.0 %fusion.35 = (f32[64,3,128]{2,1,0:T(4,128)S(1)}, f32[64,3,128]{2,1,0:T(4,128)S(1)}) fusion(f32[64,128,128]{2,1,0:T(8,128)S(1)} %fusion.34, f32[64,3,128]{2,1,0:T(4,128)S(1)} %get-tuple-element.200, f32[64,3,128]{2,1,0:T(4,128)S(1)} %get-tuple-element.201), kind=kLoop, calls=%fused_computation.8.clone.1 | loop fusion | flops 12533760 | bytes 4587520 | tf_op jit(solution)/shard_map/while/body/eval_jaxpr/reduce_sum | solution.py:23
  286.4 6.8 %scatter_fusion.1 = f32[512,3,128]{2,1,0:T(4,128)} fusion(f32[512,3,128]{2,1,0:T(4,128)} %get-tuple-element.224, s32[64]{0:T(128)S(1)} %get-tuple-element.199, f32[64,3,128]{2,1,0:T(4,128)S(1)} %neg.4), kind=kCustom, calls=%fused_computation.4.clone.1 | custom fusion | flops 24576 | bytes 295168 | tf_op jit(solution)/shard_map/while/body/eval_jaxpr/scatter-add | solution.py:74
  293.2 2.7 scatter_fusion
  296.7 2.8 gather_fusion
  299.6 13.1 %multiply_reduce_fusion.6 = (f32[64,128,128]{2,1,0:T(8,128)}, f32[64,128,128]{2,1,0:T(8,128)}, f32[64,128,128]{2,1,0:T(8,128)}) fusion(f32[64,3,128]{2,1,0:T(4,128)S(1)} %get-tuple-element.202, f32[64,3,128]{2,1,0:T(4,128)S(1)} %get-tuple-element.203, f32[64,3,128]{2,1,0:T(4,128)S(1)} %get-tuple-element.204, f32[64,3,128]{2,1,0:T(4,128)S(1)} %get-tuple-element.205), kind=kLoop, calls=%fused_computation.11.clone.1 | loop fusion | flops 15728640 | bytes 12976128 | tf_op jit(solution)/shard_map/while/body/eval_jaxpr/reduce_sum | solution.py:20
  312.6 4.1 fusion.33
  318.6 5.6 %fusion.34 = f32[64,128,128]{2,1,0:T(8,128)S(1)} fusion(f32[64,128,128]{2,1,0:T(8,128)S(1)} %fusion.33, f32[64,128,128]{2,1,0:T(8,128)} %get-tuple-element.206, f32[64,128,128]{2,1,0:T(8,128)} %get-tuple-element.207, f32[64,128,128]{2,1,0:T(8,128)S(1)} %copy-done.1, f32[64]{0:T(128)S(1)} %compare_convert_fusion.2), kind=kLoop, calls=%fused_computation.16.clone.1 | loop fusion | flops 7340032 | bytes 20971776 | tf_op jit(solution)/shard_map/while/body/eval_jaxpr/mul | solution.py:21
  324.2 8.0 %fusion.35 = (f32[64,3,128]{2,1,0:T(4,128)S(1)}, f32[64,3,128]{2,1,0:T(4,128)S(1)}) fusion(f32[64,128,128]{2,1,0:T(8,128)S(1)} %fusion.34, f32[64,3,128]{2,1,0:T(4,128)S(1)} %get-tuple-element.200, f32[64,3,128]{2,1,0:T(4,128)S(1)} %get-tuple-element.201), kind=kLoop, calls=%fused_computation.8.clone.1 | loop fusion | flops 12533760 | bytes 4587520 | tf_op jit(solution)/shard_map/while/body/eval_jaxpr/reduce_sum | solution.py:23
  332.2 6.7 %scatter_fusion.1 = f32[512,3,128]{2,1,0:T(4,128)} fusion(f32[512,3,128]{2,1,0:T(4,128)} %get-tuple-element.224, s32[64]{0:T(128)S(1)} %get-tuple-element.199, f32[64,3,128]{2,1,0:T(4,128)S(1)} %neg.4), kind=kCustom, calls=%fused_computation.4.clone.1 | custom fusion | flops 24576 | bytes 295168 | tf_op jit(solution)/shard_map/while/body/eval_jaxpr/scatter-add | solution.py:74
  338.9 2.7 scatter_fusion
  342.4 2.8 gather_fusion
  345.3 13.1 %multiply_reduce_fusion.6 = (f32[64,128,128]{2,1,0:T(8,128)}, f32[64,128,128]{2,1,0:T(8,128)}, f32[64,128,128]{2,1,0:T(8,128)}) fusion(f32[64,3,128]{2,1,0:T(4,128)S(1)} %get-tuple-element.202, f32[64,3,128]{2,1,0:T(4,128)S(1)} %get-tuple-element.203, f32[64,3,128]{2,1,0:T(4,128)S(1)} %get-tuple-element.204, f32[64,3,128]{2,1,0:T(4,128)S(1)} %get-tuple-element.205), kind=kLoop, calls=%fused_computation.11.clone.1 | loop fusion | flops 15728640 | bytes 12976128 | tf_op jit(solution)/shard_map/while/body/eval_jaxpr/reduce_sum | solution.py:20
  358.4 4.1 fusion.33
  364.3 5.6 %fusion.34 = f32[64,128,128]{2,1,0:T(8,128)S(1)} fusion(f32[64,128,128]{2,1,0:T(8,128)S(1)} %fusion.33, f32[64,128,128]{2,1,0:T(8,128)} %get-tuple-element.206, f32[64,128,128]{2,1,0:T(8,128)} %get-tuple-element.207, f32[64,128,128]{2,1,0:T(8,128)S(1)} %copy-done.1, f32[64]{0:T(128)S(1)} %compare_convert_fusion.2), kind=kLoop, calls=%fused_computation.16.clone.1 | loop fusion | flops 7340032 | bytes 20971776 | tf_op jit(solution)/shard_map/while/body/eval_jaxpr/mul | solution.py:21
  369.9 8.0 %fusion.35 = (f32[64,3,128]{2,1,0:T(4,128)S(1)}, f32[64,3,128]{2,1,0:T(4,128)S(1)}) fusion(f32[64,128,128]{2,1,0:T(8,128)S(1)} %fusion.34, f32[64,3,128]{2,1,0:T(4,128)S(1)} %get-tuple-element.200, f32[64,3,128]{2,1,0:T(4,128)S(1)} %get-tuple-element.201), kind=kLoop, calls=%fused_computation.8.clone.1 | loop fusion | flops 12533760 | bytes 4587520 | tf_op jit(solution)/shard_map/while/body/eval_jaxpr/reduce_sum | solution.py:23
  377.9 6.8 %scatter_fusion.1 = f32[512,3,128]{2,1,0:T(4,128)} fusion(f32[512,3,128]{2,1,0:T(4,128)} %get-tuple-element.224, s32[64]{0:T(128)S(1)} %get-tuple-element.199, f32[64,3,128]{2,1,0:T(4,128)S(1)} %neg.4), kind=kCustom, calls=%fused_computation.4.clone.1 | custom fusion | flops 24576 | bytes 295168 | tf_op jit(solution)/shard_map/while/body/eval_jaxpr/scatter-add | solution.py:74
  384.7 2.7 scatter_fusion
  388.2 2.8 gather_fusion
  391.1 13.1 %multiply_reduce_fusion.6 = (f32[64,128,128]{2,1,0:T(8,128)}, f32[64,128,128]{2,1,0:T(8,128)}, f32[64,128,128]{2,1,0:T(8,128)}) fusion(f32[64,3,128]{2,1,0:T(4,128)S(1)} %get-tuple-element.202, f32[64,3,128]{2,1,0:T(4,128)S(1)} %get-tuple-element.203, f32[64,3,128]{2,1,0:T(4,128)S(1)} %get-tuple-element.204, f32[64,3,128]{2,1,0:T(4,128)S(1)} %get-tuple-element.205), kind=kLoop, calls=%fused_computation.11.clone.1 | loop fusion | flops 15728640 | bytes 12976128 | tf_op jit(solution)/shard_map/while/body/eval_jaxpr/reduce_sum | solution.py:20
  404.1 4.1 fusion.33
  410.1 5.6 %fusion.34 = f32[64,128,128]{2,1,0:T(8,128)S(1)} fusion(f32[64,128,128]{2,1,0:T(8,128)S(1)} %fusion.33, f32[64,128,128]{2,1,0:T(8,128)} %get-tuple-element.206, f32[64,128,128]{2,1,0:T(8,128)} %get-tuple-element.207, f32[64,128,128]{2,1,0:T(8,128)S(1)} %copy-done.1, f32[64]{0:T(128)S(1)} %compare_convert_fusion.2), kind=kLoop, calls=%fused_computation.16.clone.1 | loop fusion | flops 7340032 | bytes 20971776 | tf_op jit(solution)/shard_map/while/body/eval_jaxpr/mul | solution.py:21
  415.7 8.0 %fusion.35 = (f32[64,3,128]{2,1,0:T(4,128)S(1)}, f32[64,3,128]{2,1,0:T(4,128)S(1)}) fusion(f32[64,128,128]{2,1,0:T(8,128)S(1)} %fusion.34, f32[64,3,128]{2,1,0:T(4,128)S(1)} %get-tuple-element.200, f32[64,3,128]{2,1,0:T(4,128)S(1)} %get-tuple-element.201), kind=kLoop, calls=%fused_computation.8.clone.1 | loop fusion | flops 12533760 | bytes 4587520 | tf_op jit(solution)/shard_map/while/body/eval_jaxpr/reduce_sum | solution.py:23
  423.7 6.7 %scatter_fusion.1 = f32[512,3,128]{2,1,0:T(4,128)} fusion(f32[512,3,128]{2,1,0:T(4,128)} %get-tuple-element.224, s32[64]{0:T(128)S(1)} %get-tuple-element.199, f32[64,3,128]{2,1,0:T(4,128)S(1)} %neg.4), kind=kCustom, calls=%fused_computation.4.clone.1 | custom fusion | flops 24576 | bytes 295168 | tf_op jit(solution)/shard_map/while/body/eval_jaxpr/scatter-add | solution.py:74
  430.4 2.7 scatter_fusion
  433.9 2.8 gather_fusion
  436.8 13.1 %multiply_reduce_fusion.6 = (f32[64,128,128]{2,1,0:T(8,128)}, f32[64,128,128]{2,1,0:T(8,128)}, f32[64,128,128]{2,1,0:T(8,128)}) fusion(f32[64,3,128]{2,1,0:T(4,128)S(1)} %get-tuple-element.202, f32[64,3,128]{2,1,0:T(4,128)S(1)} %get-tuple-element.203, f32[64,3,128]{2,1,0:T(4,128)S(1)} %get-tuple-element.204, f32[64,3,128]{2,1,0:T(4,128)S(1)} %get-tuple-element.205), kind=kLoop, calls=%fused_computation.11.clone.1 | loop fusion | flops 15728640 | bytes 12976128 | tf_op jit(solution)/shard_map/while/body/eval_jaxpr/reduce_sum | solution.py:20
  449.9 4.1 fusion.33
  455.8 5.6 %fusion.34 = f32[64,128,128]{2,1,0:T(8,128)S(1)} fusion(f32[64,128,128]{2,1,0:T(8,128)S(1)} %fusion.33, f32[64,128,128]{2,1,0:T(8,128)} %get-tuple-element.206, f32[64,128,128]{2,1,0:T(8,128)} %get-tuple-element.207, f32[64,128,128]{2,1,0:T(8,128)S(1)} %copy-done.1, f32[64]{0:T(128)S(1)} %compare_convert_fusion.2), kind=kLoop, calls=%fused_computation.16.clone.1 | loop fusion | flops 7340032 | bytes 20971776 | tf_op jit(solution)/shard_map/while/body/eval_jaxpr/mul | solution.py:21
  461.4 8.0 %fusion.35 = (f32[64,3,128]{2,1,0:T(4,128)S(1)}, f32[64,3,128]{2,1,0:T(4,128)S(1)}) fusion(f32[64,128,128]{2,1,0:T(8,128)S(1)} %fusion.34, f32[64,3,128]{2,1,0:T(4,128)S(1)} %get-tuple-element.200, f32[64,3,128]{2,1,0:T(4,128)S(1)} %get-tuple-element.201), kind=kLoop, calls=%fused_computation.8.clone.1 | loop fusion | flops 12533760 | bytes 4587520 | tf_op jit(solution)/shard_map/while/body/eval_jaxpr/reduce_sum | solution.py:23
  469.4 6.8 %scatter_fusion.1 = f32[512,3,128]{2,1,0:T(4,128)} fusion(f32[512,3,128]{2,1,0:T(4,128)} %get-tuple-element.224, s32[64]{0:T(128)S(1)} %get-tuple-element.199, f32[64,3,128]{2,1,0:T(4,128)S(1)} %neg.4), kind=kCustom, calls=%fused_computation.4.clone.1 | custom fusion | flops 24576 | bytes 295168 | tf_op jit(solution)/shard_map/while/body/eval_jaxpr/scatter-add | solution.py:74
  476.2 2.7 scatter_fusion
  481.2 5.6 %all-to-all-start.1 = ((f32[128,4,3,128]{3,1,2,0:T(4,128)}), f32[128,4,3,128]{3,1,2,0:T(4,128)S(1)}, u32[]{:S(2)}, u32[]{:S(2)}) async-start(f32[128,4,3,128]{3,1,2,0:T(4,128)} %copy.77), calls=%async_computation.1 | async-start | bytes 1572864 | tf_op jit(solution)/shard_map/all_to_all | solution.py:84
  487.6 15.7 %all-to-all-done.1 = f32[128,4,3,128]{3,1,2,0:T(4,128)S(1)} async-done(((f32[128,4,3,128]{3,1,2,0:T(4,128)}), f32[128,4,3,128]{3,1,2,0:T(4,128)S(1)}, u32[]{:S(2)}, u32[]{:S(2)}) %all-to-all-start.1) | async-done | bytes 786464 | tf_op jit(solution)/shard_map/all_to_all | solution.py:84
  504.0 16.7 %scatter_fusion.2 = f32[128,3,128]{2,1,0:T(4,128)S(1)} fusion(f32[128,3,128]{2,1,0:T(4,128)S(1)} %maximum_add_fusion, s32[512]{0:T(512)S(1)} %bitcast.50, f32[512,3,128]{2,1,0:T(4,128)S(1)} %copy.79), kind=kCustom, calls=%fused_computation.5 | custom fusion | flops 196608 | bytes 2361344 | tf_op jit(solution)/shard_map/scatter-add | solution.py:92
  (137 shorter events, 30.2 us)
Async XLA Ops:
  5.6 13.7 %copy-start = (f32[128,9,128]{2,0,1:T(8,128)S(1)}, f32[128,9,128]{2,0,1:T(8,128)}, u32[]{:S(2)}) copy-start(f32[128,9,128]{2,0,1:T(8,128)} %param.8) | copy-start | bytes 1769476
  7.4 12.3 %copy-start.2 = (s32[1,128,4]{1,2,0:T(4,128)S(1)}, s32[1,128,4]{1,2,0:T(4,128)}, u32[]{:S(2)}) copy-start(s32[1,128,4]{1,2,0:T(4,128)} %param.9) | copy-start | bytes 6148
  7.4 12.7 %copy-start.5 = (s32[128]{0:T(128)S(1)}, s32[128]{0:T(128)}, u32[]{:S(2)}) copy-start(s32[128]{0:T(128)} %param.13) | copy-start | bytes 1540
  7.4 97.4 %copy-start.3 = (s32[1,512]{1,0:T(1,128)S(1)}, s32[1,512]{1,0:T(1,128)}, u32[]{:S(2)}) copy-start(s32[1,512]{1,0:T(1,128)} %param.11) | copy-start | bytes 6148
  7.4 98.1 %copy-start.4 = (s32[1,512]{1,0:T(1,128)S(1)}, s32[1,512]{1,0:T(1,128)}, u32[]{:S(2)}) copy-start(s32[1,512]{1,0:T(1,128)} %param.10) | copy-start | bytes 6148
  7.4 98.8 %all-to-all-start = ((f32[128,4,9,128]{3,1,2,0:T(4,128)}), f32[128,4,9,128]{3,1,2,0:T(4,128)}, u32[]{:S(2)}, u32[]{:S(2)}) async-start(f32[128,4,9,128]{3,1,2,0:T(4,128)} %copy.64), calls=%async_computation | async-start | bytes 4718592 | tf_op jit(solution)/shard_map/all_to_all | solution.py:59
  129.6 5.9 %copy-start.1 = (f32[64,128,128]{2,1,0:T(8,128)S(1)}, f32[64,128,128]{2,1,0:T(8,128)}, u32[]{:S(2)}) copy-start(f32[64,128,128]{2,1,0:T(8,128)} %get-tuple-element.208) | copy-start | bytes 12582916 | tf_op jit(solution)/shard_map/while
  175.4 5.9 %copy-start.1 = (f32[64,128,128]{2,1,0:T(8,128)S(1)}, f32[64,128,128]{2,1,0:T(8,128)}, u32[]{:S(2)}) copy-start(f32[64,128,128]{2,1,0:T(8,128)} %get-tuple-element.208) | copy-start | bytes 12582916 | tf_op jit(solution)/shard_map/while
  221.1 5.9 %copy-start.1 = (f32[64,128,128]{2,1,0:T(8,128)S(1)}, f32[64,128,128]{2,1,0:T(8,128)}, u32[]{:S(2)}) copy-start(f32[64,128,128]{2,1,0:T(8,128)} %get-tuple-element.208) | copy-start | bytes 12582916 | tf_op jit(solution)/shard_map/while
  266.8 5.9 %copy-start.1 = (f32[64,128,128]{2,1,0:T(8,128)S(1)}, f32[64,128,128]{2,1,0:T(8,128)}, u32[]{:S(2)}) copy-start(f32[64,128,128]{2,1,0:T(8,128)} %get-tuple-element.208) | copy-start | bytes 12582916 | tf_op jit(solution)/shard_map/while
  312.6 5.9 %copy-start.1 = (f32[64,128,128]{2,1,0:T(8,128)S(1)}, f32[64,128,128]{2,1,0:T(8,128)}, u32[]{:S(2)}) copy-start(f32[64,128,128]{2,1,0:T(8,128)} %get-tuple-element.208) | copy-start | bytes 12582916 | tf_op jit(solution)/shard_map/while
  358.4 5.9 %copy-start.1 = (f32[64,128,128]{2,1,0:T(8,128)S(1)}, f32[64,128,128]{2,1,0:T(8,128)}, u32[]{:S(2)}) copy-start(f32[64,128,128]{2,1,0:T(8,128)} %get-tuple-element.208) | copy-start | bytes 12582916 | tf_op jit(solution)/shard_map/while
  404.1 5.9 %copy-start.1 = (f32[64,128,128]{2,1,0:T(8,128)S(1)}, f32[64,128,128]{2,1,0:T(8,128)}, u32[]{:S(2)}) copy-start(f32[64,128,128]{2,1,0:T(8,128)} %get-tuple-element.208) | copy-start | bytes 12582916 | tf_op jit(solution)/shard_map/while
  449.9 5.9 %copy-start.1 = (f32[64,128,128]{2,1,0:T(8,128)S(1)}, f32[64,128,128]{2,1,0:T(8,128)}, u32[]{:S(2)}) copy-start(f32[64,128,128]{2,1,0:T(8,128)} %get-tuple-element.208) | copy-start | bytes 12582916 | tf_op jit(solution)/shard_map/while
  481.2 22.0 %all-to-all-start.1 = ((f32[128,4,3,128]{3,1,2,0:T(4,128)}), f32[128,4,3,128]{3,1,2,0:T(4,128)S(1)}, u32[]{:S(2)}, u32[]{:S(2)}) async-start(f32[128,4,3,128]{3,1,2,0:T(4,128)} %copy.77), calls=%async_computation.1 | async-start | bytes 1572864 | tf_op jit(solution)/shard_map/all_to_all | solution.py:84
where the time goes:
time: 523 us; the launch traced here: 521 us
  other arithmetic  347 us (66%)
  blocking collectives  83.5 us (16%)
  local copies, waits for them, and re-layouts  51.5 us (10%)
  starting transfers between devices  17.5 us (3%)
  waiting for transfers between devices  15.7 us (3%)
  loops' own time  5.5 us (1%)
    reduce_sum x8, other arithmetic, interact(): jnp.sum(far_block[:, 3:6, None, :] * near_block[:, 6:9, :, None], axis=1)  105 us
    psum x1, blocking collectives, on_device(): moment_sums = lax.psum(local_moments(segments, tile_cell), ('dom', 'sub'))  83.5 us
    reduce_sum x8, other arithmetic, interact(): return (jnp.sum(weighted, axis=3), -jnp.sum(weighted, axis=2))  63.9 us
    scatter-add x8, other arithmetic, advance(): far_forces.at[remote_ids].add(far_part)  53.9 us
    mul x8, other arithmetic, interact(): (burgers_dot + cross_first * cross_second) * inverse  44.6 us
    reduce_sum x8, other arithmetic, interact(): spread = jnp.sum(apart * apart, axis=1) + core_square  32.9 us
    gather x8, local copies, waits for them, and re-layouts, advance(): arrived[remote_ids]  22.3 us
    scatter-add x8, other arithmetic, advance(): near_forces.at[local_ids].add(near_part)  21.9 us
  transfers between devices with their start and end apart: 2, of which 1 were waited for; matrix products, arithmetic and copies ran while one was open for 1% of the time, Pallas kernels for 0%

commit v1 on v0

v1 whole, which is shorter than its diff:
```python
import functools

import jax
import jax.numpy as jnp
from jax import lax
from jax.experimental import pallas as pl
from jax.experimental.pallas import tpu as pltpu
from jax.sharding import PartitionSpec as P

NCELL = 64
CAP = 4
PEERS = 128
MESH = pl.DeviceIdType.MESH
f32 = jnp.float32
bf16 = jnp.bfloat16

GROUP = 4
KNUM = 48
KDIST = 32
K = KNUM + KDIST
FROWS = K + 16
NT = (((1,), (1,)), ((), ()))


def top(v):
    return v.astype(bf16).astype(f32)


def split2(v):
    h = top(v)
    return h, v - h


def split3(v):
    h = top(v)
    r = v - h
    m = top(r)
    return h, m, r - m


def near_rows(x, b, l):
    vals = list(b) + [b[i] * l[j] for i in range(3) for j in range(3)]
    hl = [split2(v) for v in vals]
    zero = jnp.zeros_like(x[0])
    one = zero + 1.0
    num = [h for h, _ in hl] + [h for h, _ in hl] + [lo for _, lo in hl]
    num += [zero] * (KNUM - 36)
    xs = [split3(v) for v in x]
    hi, mid, low = [[s[i] for s in xs] for i in range(3)]
    q = split3(x[0] * x[0] + x[1] * x[1] + x[2] * x[2] + 0.25)
    dist = hi + hi + mid + hi + low + mid + list(q) + [one] * 3
    dist += [zero] * (KDIST - 24)
    return num + dist + list(x)


def far_rows(x, b, l):
    vals = list(b) + [l[i] * b[j] for i in range(3) for j in range(3)]
    hl = [split2(v) for v in vals]
    zero = jnp.zeros_like(x[0])
    one = zero + 1.0
    num = [h for h, _ in hl] + [lo for _, lo in hl] + [h for h, _ in hl]
    num += [zero] * (KNUM - 36)
    xs = [split3(v) for v in x]
    hi, mid, low = [[s[i] for s in xs] for i in range(3)]
    q = split3(x[0] * x[0] + x[1] * x[1] + x[2] * x[2])
    neg = lambda rows: [-2.0 * v for v in rows]
    nh, nm, nl = neg(hi), neg(mid), neg(low)
    dist = nh + nm + nh + nl + nh + nm + [one] * 3 + list(q)
    dist += [zero] * (KDIST - 24)
    two = [v - h for v, h in zip(x, hi)]
    sums = hi + [one] + [zero] * 4 + two + [zero] * 5
    return num + dist + sums


def put(scr, rows, count):
    for f, v in enumerate(rows):
        scr[8 * f : 8 * f + count, :] = v


def prepare_near(seg, nft, spread, scr):
    def body(g, carry):
        tiles = pl.ds(pl.multiple_of(g * 8, 8), 8)
        comp = [seg[tiles, a, :] for a in range(9)]
        rows = near_rows(comp[0:3], comp[3:6], comp[6:9])
        put(scr, rows, 8)
        for c in range(8):
            feat = scr[pl.ds(c, K + 8, stride=8), :]
            feat = jnp.concatenate([feat, jnp.zeros((128 - K - 8, 128), f32)], 0).T
            nft[g * 8 + c] = feat.astype(bf16)
            for a in range(3):
                spread[g * 8 + c, 128 * a : 128 * a + 128, :] = jnp.broadcast_to(
                    feat[:, K + a : K + a + 1], (128, 128)
                )
        return carry

    lax.fori_loop(0, 16, body, 0)


def block(comp, live, nears, nft, spread, scr, part):
    x, b, l = comp[0:3], [v * live for v in comp[3:6]], comp[6:9]
    put(scr, far_rows(x, b, l), CAP)
    near_parts = []
    zn = jnp.zeros((KNUM, 128), bf16)
    zd = jnp.zeros((KDIST, 128), bf16)
    for c in range(CAP):
        feat = scr[pl.ds(c, K, stride=8), :].astype(bf16)
        xf = scr[pl.ds(8 * K + c, 16, stride=8), :].astype(bf16)
        right = jnp.concatenate(
            [
                jnp.concatenate([feat[:KNUM], zn], 1),
                jnp.concatenate([zd, feat[KNUM:]], 1),
            ],
            0,
        )
        n = nears[c]
        both = jnp.dot(nft[n][:, :K], right, preferred_element_type=f32)
        inv = lax.rsqrt(both[:, 128:])
        coup = both[:, :128] * (inv * inv * inv)
        hi = coup.astype(bf16)
        lo = (coup - hi.astype(f32)).astype(bf16)
        sn = lax.dot_general(
            jnp.concatenate([xf, xf], 1),
            jnp.concatenate([hi, lo], 1),
            NT,
            preferred_element_type=f32,
        )
        near_parts.append(sn[0:8] + sn[8:16])
        acc = [None] * 4
        for i in range(16):
            cv = coup[8 * i : 8 * i + 8]
            for a in range(3):
                t = cv * spread[n, 128 * a + 8 * i : 128 * a + 8 * i + 8, :]
                acc[a] = t if acc[a] is None else acc[a] + t
            acc[3] = cv if acc[3] is None else acc[3] + cv
        for a in range(4):
            part[32 * a + 8 * c : 32 * a + 8 * c + 8, :] = acc[a]
    sums = []
    for a in range(4):
        s = part[pl.ds(32 * a, CAP, stride=8), :]
        for i in range(1, 8):
            s = s + part[pl.ds(32 * a + i, CAP, stride=8), :]
        sums.append(s)
    far = [x[a] * sums[3] - sums[a] for a in range(3)]
    return far, near_parts


def offset(j):
    k = lax.rem(j * 37, PEERS)
    return lax.rem(lax.div(k, 32), 4), lax.rem(lax.div(k, 8), 4), lax.rem(lax.div(k, 2), 4), lax.rem(k, 2)


def shifted(d, s, j, sign):
    dx, dz, dy, dc = offset(j)
    if sign < 0:
        dx, dz, dy = 4 - dx, 4 - dz, 4 - dy
    x = lax.rem(lax.div(d, 4) + dx, 4)
    z = lax.rem(lax.rem(d, 4) + dz, 4)
    y = lax.rem(lax.div(s, 2) + dy, 4)
    c = lax.rem(lax.rem(s, 2) + dc, 2)
    return x * 4 + z, y * 2 + c


def exchange(
    near_ref, live_ref, send_ref, seg_hbm, mom_ref,
    nraw_ref, back_ref, total_ref,
    seg, stage, recv, back, nft, spread, nscr, scr, part, mom_a, mom_b,
    seg_sem, out_send, out_recv, back_send, back_recv, mom_sem, stage_sem,
):
    d = lax.axis_index("dom")
    s = lax.axis_index("sub")
    barrier = pltpu.get_barrier_semaphore()
    for k in range(1, 8):
        pl.semaphore_signal(barrier, inc=1, device_id=(d, lax.rem(s + k, 8)), device_id_type=MESH)
    for k in range(1, 16):
        pl.semaphore_signal(barrier, inc=1, device_id=(lax.rem(d + k, 16), s), device_id_type=MESH)
    load = pltpu.make_async_copy(seg_hbm, seg, seg_sem)
    load.start()
    load.wait()

    def gather(j, carry):
        td, ts = shifted(d, s, j, 1)
        base = (td * 8 + ts) * CAP
        for c in range(CAP):
            stage[j, 9 * c : 9 * c + 9, :] = seg[send_ref[base + c]]
        return carry

    lax.fori_loop(0, PEERS, gather, 0)
    recv[0] = stage[0]
    mom_a[0] = mom_ref[...]

    pl.semaphore_wait(barrier, 22)
    for k in range(1, 8):
        pl.semaphore_signal(stage_sem, inc=1, device_id=(d, lax.rem(s + k, 8)), device_id_type=MESH)
    pl.semaphore_wait(stage_sem, 7)

    def mom_copy_a(k):
        return pltpu.make_async_remote_copy(
            src_ref=mom_ref, dst_ref=mom_a.at[k], send_sem=mom_sem.at[0], recv_sem=mom_sem.at[1],
            device_id=(d, lax.rem(s + k, 8)), device_id_type=MESH)

    def mom_copy_b(k):
        return pltpu.make_async_remote_copy(
            src_ref=mom_b.at[0], dst_ref=mom_b.at[k], send_sem=mom_sem.at[2], recv_sem=mom_sem.at[3],
            device_id=(lax.rem(d + k, 16), s), device_id_type=MESH)

    for k in range(1, 8):
        mom_copy_a(k).start()

    def send(j, carry):
        pltpu.make_async_remote_copy(
            src_ref=stage.at[j], dst_ref=recv.at[j], send_sem=out_send, recv_sem=out_recv.at[lax.div(j, GROUP)],
            device_id=shifted(d, s, j, 1), device_id_type=MESH).start()
        return carry

    lax.fori_loop(1, PEERS, send, 0)
    prepare_near(seg, nft, spread, nscr)

    a_all = pltpu.make_async_remote_copy(
        src_ref=mom_a.at[pl.ds(1, 7)], dst_ref=mom_a.at[pl.ds(1, 7)], send_sem=mom_sem.at[0], recv_sem=mom_sem.at[1],
        device_id=(d, lax.rem(s + 1, 8)), device_id_type=MESH)
    a_all.wait_recv()
    mom_b[0] = jnp.sum(mom_a[...], 0)
    for k in range(1, 16):
        mom_copy_b(k).start()

    def wait_blocks(first, count, g):
        pltpu.make_async_remote_copy(
            src_ref=stage.at[pl.ds(first, count)], dst_ref=recv.at[pl.ds(first, count)],
            send_sem=out_send, recv_sem=out_recv.at[g],
            device_id=shifted(d, s, 1, 1), device_id_type=MESH).wait_recv()

    def back_copy(j):
        return pltpu.make_async_remote_copy(
            src_ref=stage.at[j, pl.ds(0, 12)], dst_ref=back.at[j], send_sem=back_send, recv_sem=back_recv,
            device_id=shifted(d, s, j, -1), device_id_type=MESH)

    rows = lax.broadcasted_iota(jnp.int32, (CAP, 128), 0)

    def work(g, carry):
        @pl.when(g == 0)
        def _():
            wait_blocks(1, GROUP - 1, 0)

        @pl.when(g > 0)
        def _():
            wait_blocks(g * GROUP, GROUP, g)

        for u in range(GROUP):
            j = g * GROUP + u
            td, ts = shifted(d, s, j, -1)
            base = (td * 8 + ts) * CAP
            comp = [recv[j, pl.ds(a, CAP, stride=9), :] for a in range(9)]
            live = jnp.full((CAP, 128), live_ref[base], f32)
            for c in range(1, CAP):
                live = jnp.where(rows == c, live_ref[base + c], live)
            nears = [near_ref[base + c] for c in range(CAP)]
            far, near = block(comp, live, nears, nft, spread, scr.at[u], part.at[u])
            for a in range(3):
                recv[j, CAP * a : CAP * a + CAP, :] = far[a]
            for c in range(CAP):
                nraw_ref[j, 4 * c : 4 * c + 4, :] = near[c][0:4]

        for u in range(GROUP):
            j = g * GROUP + u

            @pl.when(j > 0)
            def _():
                pltpu.make_async_remote_copy(
                    src_ref=recv.at[j, pl.ds(0, 12)], dst_ref=back.at[j], send_sem=back_send, recv_sem=back_recv,
                    device_id=shifted(d, s, j, -1), device_id_type=MESH).start()

        return carry

    lax.fori_loop(0, PEERS // GROUP, work, 0)
    back[0] = recv[0, 0:12, :]
    a_all.wait_send()
    b_all = pltpu.make_async_remote_copy(
        src_ref=mom_b.at[pl.ds(1, 15)], dst_ref=mom_b.at[pl.ds(1, 15)], send_sem=mom_sem.at[2], recv_sem=mom_sem.at[3],
        device_id=(lax.rem(d + 1, 16), s), device_id_type=MESH)
    b_all.wait()
    total_ref[...] = jnp.sum(mom_b[...], 0)
    pltpu.make_async_remote_copy(
        src_ref=stage.at[pl.ds(1, PEERS - 1)], dst_ref=recv.at[pl.ds(1, PEERS - 1)], send_sem=out_send,
        recv_sem=out_recv.at[0], device_id=shifted(d, s, 1, 1), device_id_type=MESH).wait_send()
    pltpu.make_async_remote_copy(
        src_ref=back.at[pl.ds(1, PEERS - 1)], dst_ref=back.at[pl.ds(1, PEERS - 1)], send_sem=back_send,
        recv_sem=back_recv, device_id=shifted(d, s, 1, 1), device_id_type=MESH).wait()
    back_ref[...] = back[...]


def run_exchange(near_of, live, send_flat, segments, mom):
    vm = pl.BlockSpec(memory_space=pltpu.VMEM)
    sm = pl.BlockSpec(memory_space=pltpu.SMEM)
    dma = pltpu.SemaphoreType.DMA
    return pl.pallas_call(
        exchange,
        out_shape=(
            jax.ShapeDtypeStruct((PEERS, 16, 128), f32),
            jax.ShapeDtypeStruct((PEERS, 12, 128), f32),
            jax.ShapeDtypeStruct((8, 128), f32),
        ),
        in_specs=[sm, sm, sm, pl.BlockSpec(memory_space=pl.ANY), vm],
        out_specs=(vm, vm, vm),
        scratch_shapes=[
            pltpu.VMEM((128, 9, 128), f32),
            pltpu.VMEM((PEERS, 36, 128), f32),
            pltpu.VMEM((PEERS, 36, 128), f32),
            pltpu.VMEM((PEERS, 12, 128), f32),
            pltpu.VMEM((128, 128, 128), bf16),
            pltpu.VMEM((128, 384, 128), f32),
            pltpu.VMEM((8 * (K + 8), 128), f32),
            pltpu.VMEM((GROUP, 8 * FROWS, 128), f32),
            pltpu.VMEM((GROUP, 128, 128), f32),
            pltpu.VMEM((8, 8, 128), f32),
            pltpu.VMEM((16, 8, 128), f32),
            dma(()),
            dma(()),
            dma((PEERS // GROUP,)),
            dma(()),
            dma(()),
            dma((4,)),
            pltpu.SemaphoreType.REGULAR,
        ],
        compiler_params=pltpu.CompilerParams(
            collective_id=0, has_side_effects=True, vmem_limit_bytes=58 << 20
        ),
    )(near_of, live, send_flat, segments, mom)


def collect(near_ref, send_ref, nraw, back, seg, out, acc, accf):
    d = lax.axis_index("dom")
    s = lax.axis_index("sub")
    acc[...] = jnp.zeros_like(acc)
    accf[...] = jnp.zeros_like(accf)

    def add(j, carry):
        nd, ns = shifted(d, s, j, -1)
        fd, fs = shifted(d, s, j, 1)
        for c in range(CAP):
            n = near_ref[(nd * 8 + ns) * CAP + c]
            acc[n] += nraw[j, 4 * c : 4 * c + 4, :]
            t = send_ref[(fd * 8 + fs) * CAP + c]
            accf[t, 0:3, :] += back[j, pl.ds(c, 3, stride=CAP), :]
        return carry

    lax.fori_loop(0, PEERS, add, 0)

    def finish(t, carry):
        out[t] = seg[t, 0:3, :] * acc[t, 3:4, :] - acc[t, 0:3, :] + accf[t, 0:3, :]
        return carry

    lax.fori_loop(0, 128, finish, 0)


def run_collect(near_of, send_flat, nraw, back, segments):
    vm = pl.BlockSpec(memory_space=pltpu.VMEM)
    sm = pl.BlockSpec(memory_space=pltpu.SMEM)
    return pl.pallas_call(
        collect,
        out_shape=jax.ShapeDtypeStruct((128, 3, 128), f32),
        in_specs=[sm, sm, vm, vm, vm],
        out_specs=vm,
        scratch_shapes=[pltpu.VMEM((128, 4, 128), f32), pltpu.VMEM((128, 4, 128), f32)],
        compiler_params=pltpu.CompilerParams(vmem_limit_bytes=32 << 20),
    )(near_of, send_flat, nraw, back, segments)


def far_field(segments, tile_cell, moment_sums, total_segments):
    moments = moment_sums.reshape(NCELL, 3, 3) / jnp.sqrt(jnp.float32(total_segments))
    moments = 0.5 * (moments + jnp.transpose(moments, (0, 2, 1)))
    cells = jnp.arange(NCELL).astype(jnp.float32)
    weights = 8.0 / (8.0 + jnp.abs(cells[:, None] - cells[None, :]))
    stress = jnp.dot(weights, moments.reshape(NCELL, 9), precision=lax.Precision.HIGHEST)
    onehot = (tile_cell[:, None] == jnp.arange(NCELL)[None, :]).astype(jnp.float32)
    tile_stress = jnp.dot(onehot, stress, precision=lax.Precision.HIGHEST).reshape(-1, 3, 3)
    traction = jnp.sum(tile_stress[:, :, :, None] * segments[:, None, 3:6, :], axis=2)
    lines = segments[:, 6:9, :]
    return jnp.stack(
        [
            traction[:, 1] * lines[:, 2] - traction[:, 2] * lines[:, 1],
            traction[:, 2] * lines[:, 0] - traction[:, 0] * lines[:, 2],
            traction[:, 0] * lines[:, 1] - traction[:, 1] * lines[:, 0],
        ],
        axis=1,
    )


def local_moments(segments, tile_cell):
    outer = jnp.sum(segments[:, 3:6, None, :] * segments[:, None, 6:9, :], axis=3).reshape(-1, 9)
    onehot = (jnp.arange(NCELL)[:, None] == tile_cell[None, :]).astype(jnp.float32)
    return jnp.dot(onehot, outer, precision=lax.Precision.HIGHEST)


def on_device(segments, send_tiles, pair_local, pair_remote, pair_count, tile_cell):
    width = segments.shape[2]
    slots = pair_remote.shape[1]
    here = pair_remote[0][None, :] == jnp.arange(slots, dtype=jnp.int32)[:, None]
    alive = (jnp.arange(slots) < pair_count[0]).astype(jnp.int32)
    code = jnp.sum(jnp.where(here, (pair_local[0] + 128 * alive)[None, :], 0), axis=1)
    near_of = lax.rem(code, 128)
    live = lax.div(code, 128).astype(f32)
    send_flat = send_tiles.reshape(-1)
    mom = local_moments(segments, tile_cell).reshape(-1)
    mom = jnp.concatenate([mom, jnp.zeros((1024 - mom.shape[0],), f32)]).reshape(8, 128)
    nraw, back, total = run_exchange(near_of, live, send_flat, segments, mom)
    pair_forces = run_collect(near_of, send_flat, nraw, back, segments)
    moment_sums = total.reshape(-1)[: NCELL * 9].reshape(NCELL, 9)
    total_segments = segments.shape[0] * width * PEERS
    return pair_forces + far_field(segments, tile_cell, moment_sums, total_segments)


def solution(mesh):
    in_specs = (
        P(("dom", "sub"), None, None),
        P(("dom", "sub"), None, None),
        P(("dom", "sub"), None),
        P(("dom", "sub"), None),
        P(("dom", "sub")),
        P(("dom", "sub")),
    )
    out_specs = P(("dom", "sub"), None, None)
    return jax.shard_map(
        on_device, mesh=mesh, in_specs=in_specs, out_specs=out_specs, check_vma=False
    )
```

time: 523 us -> 90.1 us (0.17)
  other arithmetic: 347 us -> 2.55 us
  blocking collectives: 83.5 us -> 0 us
  Pallas kernels: 0 us -> 77 us
  local copies, waits for them, and re-layouts: 51.5 us -> 8.72 us
  starting transfers between devices: 17.5 us -> 0 us
  waiting for transfers between devices: 15.7 us -> 0 us
  loops' own time: 5.5 us -> 0 us
    reduce_sum x24 -> x1, other arithmetic: 201 us -> 0.19 us  [on_device(): jnp.sum(jnp.where(here, (pair_local[0] + 128 * alive)[None, :], 0), axis=1)]
    scatter-add x17 -> x0, other arithmetic: 92.6 us -> none  [the longest x8 53.9 us: advance(): far_forces.at[remote_ids].add(far_part)]
    psum x1 -> x0, blocking collectives: 83.5 us -> none  [on_device(): moment_sums = lax.psum(local_moments(segments, tile_cell), ('dom', 'sub'))]
    pallas_call x0 -> x2, Pallas kernels: none -> 77 us  [the longest x1 68.9 us: run_exchange(): pl.pallas_call(exchange, out_shape=(jax.ShapeDtypeStruct((PEERS, 16, 128)...]
    mul x8 -> x0, other arithmetic: 44.6 us -> none  [interact(): (burgers_dot + cross_first * cross_second) * inverse]
    gather x18 -> x0, local copies, waits for them, and re-layouts: 33.7 us -> none  [the longest x8 22.3 us: advance(): arrived[remote_ids]]
    all_to_all x2 -> x0, starting transfers between devices: 17.5 us -> none  [the longest x1 11.9 us: on_device(): lax.all_to_all(outgoing, ('dom', 'sub'), split_axis=0, concat_axis=0, til...]
    all_to_all x2 -> x0, waiting for transfers between devices: 15.7 us -> none  [the longest x1 15.7 us: on_device(): lax.all_to_all(far_forces.reshape(peers, slots, 3, width), ('dom', 'sub')...]
  transfers between devices with their start and end apart: 2 -> 0, of which waited for: 1 -> 0; matrix products, arithmetic and copies ran while one was open for 1% -> 0% of each run, Pallas kernels for 0% -> 0%
where the time goes in v1:
time: 90.1 us; the launch traced here: 89.7 us
  Pallas kernels  77 us (85%)
  local copies, waits for them, and re-layouts  8.72 us (10%)
  other arithmetic  2.55 us (3%)
    pallas_call x1, Pallas kernels, run_exchange(): pl.pallas_call(exchange, out_shape=(jax.ShapeDtypeStruct((PEERS, 16, 128)...  68.9 us
    pallas_call x1, Pallas kernels, run_collect(): pl.pallas_call(collect, out_shape=jax.ShapeDtypeStruct((128, 3, 128), f32...  8.14 us
    unnamed x22, local copies, waits for them, and re-layouts  4.66 us

profile of v1, /device:TPU:1, one launch (start us, length us, event | category | flops | bytes accessed | tf_op | source)
XLA Modules:
  0.0 89.7 jit_solution(404486695267634086)
XLA Ops:
  0.0 0.0 copy-start.5
  0.0 1.1 %fusion.12 = (f32[128,3,128]{2,0,1:T(8,128)S(1)}, f32[128,3,128]{2,0,1:T(8,128)S(1)}) fusion(f32[128,9,128]{2,0,1:T(8,128)} %param.6), kind=kLoop, calls=%fused_computation.31 | loop fusion | bytes 786432 | tf_op jit(solution)/shard_map/slice | solution.py:389
  1.1 0.3 multiply_reduce_fusion.1
  1.4 0.0 copy-start.9
  1.4 0.6 copy-done.9
  2.0 0.1 fusion.4
  2.2 0.1 reshape.46
  2.3 0.6 pad_bitcast_fusion.mom_ref
  2.9 0.0 copy-done.5
  2.9 0.0 copy-start.7
  2.9 1.3 %copy.34.seg_hbm.seg = f32[128,9,128]{2,1,0:T(8,128)} copy(f32[128,9,128]{2,0,1:T(8,128)S(1)} %copy-done.5) | data formatting | bytes 1179648 | tf_op args[0]
  4.3 0.0 copy-start.8
  4.9 0.0 copy-done.8
  4.9 0.0 copy-start.6
  5.0 0.7 copy-done.6
  5.6 0.2 select_reduce_fusion
  5.8 0.6 fusion.9
  6.4 0.0 copy-done.7
  6.4 0.1 copy.32
  6.5 0.7 reshape.44.send_ref
  7.2 68.9 %shard_map.64 = (f32[128,16,128]{2,1,0:T(8,128)}, f32[128,12,128]{2,1,0:T(8,128)}, f32[8,128]{1,0:T(8,128)}) custom-call(s32[512]{0:T(512)} %get-tuple-element.20.near_ref, f32[512]{0:T(512)} %get-tuple-element.19.live_ref, s32[512]{0:T(512)} %reshape.44.send_ref, f32[128,9,128]{2,1,0:T(8,128)} %copy.34.seg_hbm.seg, f32[8,128]{1,0:T(8,128)} %pad_bitcast_fusion.mom_ref), custom_call_target="tpu_custom_call" | custom-call | tf_op jit(solution)/shard_map/pallas_call | solution.py:295
  76.0 0.0 copy-start
  76.1 0.8 slice_multiply_fusion
  76.8 0.2 div.27
  77.1 0.5 copy.36
  77.6 0.0 copy-start.1
  77.6 0.1 copy.37
  77.7 0.2 fusion.2
  78.0 0.2 fusion.1
  78.2 0.3 multiply_reduce_fusion
  78.5 0.0 copy-done
  78.5 0.2 multiply_subtract_fusion.2
  78.8 0.0 copy-start.4
  78.8 0.0 copy-start.3
  78.8 0.0 copy-done.1
  78.8 0.6 copy-done.4
  79.4 0.0 copy-done.3
  79.4 0.0 copy-start.2
  79.4 1.2 %copy-done.2 = f32[128,12,128]{2,1,0:T(8,128)S(1)} copy-done((f32[128,12,128]{2,1,0:T(8,128)S(1)}, f32[128,12,128]{2,1,0:T(8,128)}, u32[]{:S(2)}) %copy-start.2) | copy-done | bytes 786456
  80.6 8.1 %shard_map.65 = f32[128,3,128]{2,1,0:T(4,128)S(1)} custom-call(s32[512]{0:T(512)S(1)} %copy-done.3, s32[512]{0:T(512)S(1)} %copy-done.4, f32[128,16,128]{2,1,0:T(8,128)S(1)} %copy-done.1, f32[128,12,128]{2,1,0:T(8,128)S(1)} %copy-done.2, f32[128,9,128]{2,1,0:T(8,128)S(1)} %copy-done), custom_call_target="tpu_custom_call" | custom-call | tf_op jit(solution)/shard_map/pallas_call | solution.py:358
  88.8 0.2 maximum_add_fusion
  89.0 0.7 copy.44
  (7 shorter events, 0.1 us)
Async XLA Ops:
  0.0 2.9 %copy-start.5 = (f32[128,9,128]{2,0,1:T(8,128)S(1)}, f32[128,9,128]{2,0,1:T(8,128)}, u32[]{:S(2)}) copy-start(f32[128,9,128]{2,0,1:T(8,128)} %param.6) | copy-start | bytes 1769476
  1.4 0.7 copy-start.9
  2.9 3.5 %copy-start.7 = (s32[1,128,4]{1,2,0:T(4,128)S(1)}, s32[1,128,4]{1,2,0:T(4,128)}, u32[]{:S(2)}) copy-start(s32[1,128,4]{1,2,0:T(4,128)} %param.7) | copy-start | bytes 6148
  4.3 0.7 copy-start.8
  4.9 0.7 copy-start.6
  76.0 2.5 %copy-start = (f32[128,9,128]{2,1,0:T(8,128)S(1)}, f32[128,9,128]{2,1,0:T(8,128)}, u32[]{:S(2)}) copy-start(f32[128,9,128]{2,1,0:T(8,128)} %copy.34.seg_hbm.seg) | copy-start | bytes 1769476
  77.6 1.2 %copy-start.1 = (f32[128,16,128]{2,1,0:T(8,128)S(1)}, f32[128,16,128]{2,1,0:T(8,128)}, u32[]{:S(2)}) copy-start(f32[128,16,128]{2,1,0:T(8,128)} %get-tuple-element.8.nraw) | copy-start | bytes 3145732
  78.8 0.6 copy-start.4
  78.8 0.6 copy-start.3
  79.4 1.2 %copy-start.2 = (f32[128,12,128]{2,1,0:T(8,128)S(1)}, f32[128,12,128]{2,1,0:T(8,128)}, u32[]{:S(2)}) copy-start(f32[128,12,128]{2,1,0:T(8,128)} %get-tuple-element.9.back) | copy-start | bytes 2359300

commit v2 on v1

v2 whole, which is shorter than its diff:
```python
import math

import jax
import jax.numpy as jnp
from jax import lax
from jax.experimental import pallas as pl
from jax.experimental.pallas import tpu as pltpu
from jax.sharding import PartitionSpec as P

NCELL = 64
CAP = 4
PEERS = 128
MESH = pl.DeviceIdType.MESH
f32 = jnp.float32
bf16 = jnp.bfloat16

GROUP = 8
KNUM = 48
KDIST = 32
K = KNUM + KDIST
FROWS = K + 16
NT = (((1,), (1,)), ((), ()))
EXACT = lax.Precision.HIGHEST


def top(v):
    return v.astype(bf16).astype(f32)


def split2(v):
    h = top(v)
    return h, v - h


def split3(v):
    h = top(v)
    r = v - h
    m = top(r)
    return h, m, r - m


def near_rows(x, b, l):
    vals = list(b) + [b[i] * l[j] for i in range(3) for j in range(3)]
    hl = [split2(v) for v in vals]
    zero = jnp.zeros_like(x[0])
    one = zero + 1.0
    num = [h for h, _ in hl] + [h for h, _ in hl] + [lo for _, lo in hl]
    num += [zero] * (KNUM - 36)
    xs = [split3(v) for v in x]
    hi, mid, low = [[s[i] for s in xs] for i in range(3)]
    q = split3(x[0] * x[0] + x[1] * x[1] + x[2] * x[2] + 0.25)
    dist = hi + hi + mid + hi + low + mid + list(q) + [one] * 3
    dist += [zero] * (KDIST - 24)
    return num + dist


def far_rows(x, b, l):
    vals = list(b) + [l[i] * b[j] for i in range(3) for j in range(3)]
    hl = [split2(v) for v in vals]
    zero = jnp.zeros_like(x[0])
    one = zero + 1.0
    num = [h for h, _ in hl] + [lo for _, lo in hl] + [h for h, _ in hl]
    num += [zero] * (KNUM - 36)
    xs = [split3(v) for v in x]
    hi, mid, low = [[s[i] for s in xs] for i in range(3)]
    q = split3(x[0] * x[0] + x[1] * x[1] + x[2] * x[2])
    neg = lambda rows: [-2.0 * v for v in rows]
    nh, nm, nl = neg(hi), neg(mid), neg(low)
    dist = nh + nm + nh + nl + nh + nm + [one] * 3 + list(q)
    dist += [zero] * (KDIST - 24)
    rest = [v - h for v, h in zip(x, hi)]
    sums = hi + [one] + [zero] * 4 + rest + [zero] * 5
    return num + dist + sums


def put(scr, rows):
    for f, v in enumerate(rows):
        scr[8 * f : 8 * f + 8, :] = v


def prepare_near(seg, nft, spread, scr):
    k = lax.broadcasted_iota(jnp.int32, (K, 384), 0) - KNUM
    a = lax.broadcasted_iota(jnp.int32, (K, 384), 1) // 128
    pick = (k == a) | (k == a + 6) | (k == a + 12)
    pick = jnp.where(pick, 1.0, 0.0).astype(bf16)

    def body(g, carry):
        tiles = pl.ds(pl.multiple_of(g * 8, 8), 8)
        comp = [seg[i, tiles, :] for i in range(9)]
        put(scr, near_rows(comp[0:3], comp[3:6], comp[6:9]))
        for c in range(8):
            feat = scr[pl.ds(c, K, stride=8), :]
            feat = jnp.concatenate([feat, jnp.zeros((128 - K, 128), f32)], 0).T.astype(bf16)
            nft[g * 8 + c] = feat
            wide = jnp.dot(feat[:, :K], pick, preferred_element_type=f32)
            for i in range(3):
                spread[g * 8 + c, 128 * i : 128 * i + 128, :] = wide[:, 128 * i : 128 * i + 128]
        return carry

    lax.fori_loop(0, 16, body, 0)
    lane = lax.broadcasted_iota(jnp.int32, (128, 128), 1)
    nft[128] = jnp.where(lane == KNUM + 18, 1.0, 0.0).astype(bf16)
    spread[128] = jnp.zeros((384, 128), f32)


def block(comp, nears, nft, spread, scr, part):
    x, b, l = comp[0:3], comp[3:6], comp[6:9]
    put(scr, far_rows(x, b, l))
    near_parts = []
    zn = jnp.zeros((KNUM, 128), bf16)
    zd = jnp.zeros((KDIST, 128), bf16)
    for c in range(8):
        feat = scr[pl.ds(c, K, stride=8), :].astype(bf16)
        xf = scr[pl.ds(8 * K + c, 16, stride=8), :].astype(bf16)
        right = jnp.concatenate(
            [
                jnp.concatenate([feat[:KNUM], zn], 1),
                jnp.concatenate([zd, feat[KNUM:]], 1),
            ],
            0,
        )
        n = nears[c]
        both = jnp.dot(nft[n][:, :K], right, preferred_element_type=f32)
        inv = lax.rsqrt(both[:, 128:])
        coup = both[:, :128] * (inv * inv * inv)
        hi = coup.astype(bf16)
        lo = (coup - hi.astype(f32)).astype(bf16)
        sn = lax.dot_general(
            jnp.concatenate([xf, xf], 1),
            jnp.concatenate([hi, lo], 1),
            NT,
            preferred_element_type=f32,
        )
        near_parts.append(sn[0:8] + sn[8:16])
        acc = [None] * 4
        for i in range(16):
            cv = coup[8 * i : 8 * i + 8]
            for a in range(3):
                t = cv * spread[n, 128 * a + 8 * i : 128 * a + 8 * i + 8, :]
                acc[a] = t if acc[a] is None else acc[a] + t
            acc[3] = cv if acc[3] is None else acc[3] + cv
        for a in range(4):
            part[64 * a + 8 * c : 64 * a + 8 * c + 8, :] = acc[a]
    sums = []
    for a in range(4):
        s = part[pl.ds(64 * a, 8, stride=8), :]
        for i in range(1, 8):
            s = s + part[pl.ds(64 * a + i, 8, stride=8), :]
        sums.append(s)
    far = [x[a] * sums[3] - sums[a] for a in range(3)]
    return far, near_parts


def shifted(d, s, j, sign):
    k = (j * 37) & 127
    dx, dz, dy = k >> 5, (k >> 3) & 3, (k >> 1) & 3
    if sign < 0:
        dx, dz, dy = 4 - dx, 4 - dz, 4 - dy
    x = ((d >> 2) + dx) & 3
    z = ((d & 3) + dz) & 3
    y = ((s >> 1) + dy) & 3
    c = ((s & 1) + (k & 1)) & 1
    return x * 4 + z, y * 2 + c


def exchange(
    send_smem, seg_hbm, send_ref, local_ref, remote_ref, count_ref, cell_ref,
    out_ref,
    seg, tiles, stage, recv, back, nraw, nft, spread, nscr, scr, part, mom, mom_a, mom_b, nrow, near_smem,
    seg_sem, out_send, out_recv, back_send, back_recv, mom_sem, row_sem, stage_sem,
):
    d = lax.axis_index("dom")
    s = lax.axis_index("sub")
    me = d * 8 + s
    barrier = pltpu.get_barrier_semaphore()
    for k in range(1, 8):
        pl.semaphore_signal(barrier, inc=1, device_id=(d, (s + k) & 7), device_id_type=MESH)
    for k in range(1, 16):
        pl.semaphore_signal(barrier, inc=1, device_id=((d + k) & 15, s), device_id_type=MESH)
    load = pltpu.make_async_copy(seg_hbm, seg, seg_sem)
    load.start()

    remote = remote_ref[...]
    slot = (remote & 3) * 128 + (remote >> 2)
    pair = lax.broadcasted_iota(jnp.int32, (1, 512), 1)
    value = jnp.where(pair < count_ref[0], local_ref[...], 128).astype(f32).astype(bf16)
    value = jnp.broadcast_to(value, (16, 512))
    rows = lax.broadcasted_iota(jnp.int32, (128, 512), 0)
    for c in range(CAP):
        here = jnp.where(rows + 128 * c == slot, 1.0, 0.0).astype(bf16)
        row = lax.dot_general(value, here, NT, preferred_element_type=f32)
        nrow[c : c + 1, :] = jnp.clip(row[0:1].astype(jnp.int32), 0, 128)
    nrow[4:8, :] = jnp.zeros((4, 128), jnp.int32)
    to_smem = pltpu.make_async_copy(nrow, near_smem, row_sem)
    to_smem.start()

    load.wait()
    for g in range(16):
        for a in range(9):
            tiles[8 * g : 8 * g + 8, a, :] = seg[a, 8 * g : 8 * g + 8, :]

    def gather(j, carry):
        td, ts = shifted(d, s, j, 1)
        there = td * 8 + ts
        for c in range(CAP):
            stage[j, 9 * c : 9 * c + 9, :] = tiles[send_smem[c, there]]
        return carry

    lax.fori_loop(0, PEERS, gather, 0)
    recv[0:36, :] = stage[0]

    lane = lax.broadcasted_iota(jnp.int32, (128, 128), 1)
    cells = lax.broadcasted_iota(jnp.int32, (128, 128), 0)
    onehot = jnp.where(cells == cell_ref[...], 1.0, 0.0)
    outer = jnp.zeros((128, 128), f32)
    for a in range(3):
        for b in range(3):
            total = jnp.sum(seg[3 + a] * seg[6 + b], axis=1, keepdims=True)
            outer = jnp.where(lane == 3 * a + b, total, outer)
    mom[...] = jnp.dot(onehot, outer, precision=EXACT, preferred_element_type=f32).T[0:16]
    mom_a[0] = mom[...]

    pl.semaphore_wait(barrier, 22)
    for k in range(1, 8):
        pl.semaphore_signal(stage_sem, inc=1, device_id=(d, (s + k) & 7), device_id_type=MESH)
    pl.semaphore_wait(stage_sem, 7)

    for k in range(1, 8):
        pltpu.make_async_remote_copy(
            src_ref=mom, dst_ref=mom_a.at[k], send_sem=mom_sem.at[0], recv_sem=mom_sem.at[1],
            device_id=(d, (s + k) & 7), device_id_type=MESH).start()

    def send(j, carry):
        pltpu.make_async_remote_copy(
            src_ref=stage.at[j], dst_ref=recv.at[pl.ds(pl.multiple_of(j * 40, 8), 36)],
            send_sem=out_send, recv_sem=out_recv.at[j // GROUP],
            device_id=shifted(d, s, j, 1), device_id_type=MESH).start()
        return carry

    lax.fori_loop(1, PEERS, send, 0)
    prepare_near(seg, nft, spread, nscr)

    a_all = pltpu.make_async_remote_copy(
        src_ref=mom_a.at[pl.ds(1, 7)], dst_ref=mom_a.at[pl.ds(1, 7)], send_sem=mom_sem.at[0], recv_sem=mom_sem.at[1],
        device_id=(d, (s + 1) & 7), device_id_type=MESH)
    a_all.wait()
    mom_b[0] = jnp.sum(mom_a[...], 0)
    for k in range(1, 16):
        pltpu.make_async_remote_copy(
            src_ref=mom_b.at[0], dst_ref=mom_b.at[k], send_sem=mom_sem.at[2], recv_sem=mom_sem.at[3],
            device_id=((d + k) & 15, s), device_id_type=MESH).start()
    to_smem.wait()

    def wait_blocks(count, g):
        pltpu.make_async_remote_copy(
            src_ref=stage.at[pl.ds(0, count)], dst_ref=stage.at[pl.ds(0, count)],
            send_sem=out_send, recv_sem=out_recv.at[g],
            device_id=shifted(d, s, 1, 1), device_id_type=MESH).wait_recv()

    low = lax.broadcasted_iota(jnp.int32, (8, 128), 0) < CAP

    def work(g, carry):
        @pl.when(g == 0)
        def _():
            wait_blocks(GROUP - 1, 0)

        @pl.when(g > 0)
        def _():
            wait_blocks(GROUP, g)

        for u in range(GROUP // 2):
            j = g * GROUP + 2 * u
            first = pl.multiple_of(j * 40, 8)
            comp = []
            for a in range(9):
                even = recv[pl.ds(first + a, 8, stride=9), :]
                odd = recv[pl.ds(first + 4 + a, 8, stride=9), :]
                comp.append(jnp.where(low, even, odd))
            who = []
            for v in range(2):
                td, ts = shifted(d, s, j + v, -1)
                who.append(td * 8 + ts)
            nears = [jnp.clip(near_smem[c, who[v]], 0, 128) for v in range(2) for c in range(CAP)]
            far, near = block(comp, nears, nft, spread, scr.at[u], part.at[u])
            for v in range(2):
                for a in range(3):
                    recv[pl.ds(first + 40 * v + CAP * a, CAP), :] = far[a][CAP * v : CAP * v + CAP]
                for c in range(CAP):
                    nraw[pl.ds(pl.multiple_of(who[v] * 16, 16) + 4 * c, 4), :] = near[CAP * v + c][0:4]

        for u in range(GROUP):
            j = g * GROUP + u

            @pl.when(j > 0)
            def _():
                pltpu.make_async_remote_copy(
                    src_ref=recv.at[pl.ds(pl.multiple_of(j * 40, 8), 12)],
                    dst_ref=back.at[pl.ds(pl.multiple_of(me * 16, 16), 12)],
                    send_sem=back_send, recv_sem=back_recv,
                    device_id=shifted(d, s, j, -1), device_id_type=MESH).start()

        return carry

    lax.fori_loop(0, PEERS // GROUP, work, 0)
    back[pl.ds(pl.multiple_of(me * 16, 16), 12), :] = recv[0:12, :]

    b_all = pltpu.make_async_remote_copy(
        src_ref=mom_b.at[pl.ds(1, 15)], dst_ref=mom_b.at[pl.ds(1, 15)], send_sem=mom_sem.at[2], recv_sem=mom_sem.at[3],
        device_id=((d + 1) & 15, s), device_id_type=MESH)
    b_all.wait()
    sums = jnp.sum(mom_b[...], 0)
    scale = 0.5 / math.sqrt(PEERS * 128 * 128)
    sym = [(sums[3 * a + b : 3 * a + b + 1] + sums[3 * b + a : 3 * b + a + 1]) * scale for a in range(3) for b in range(3)]
    moments = jnp.concatenate(sym + [jnp.zeros((128 - 9, 128), f32)], 0).T
    rows = lax.broadcasted_iota(jnp.int32, (128, 128), 0)
    lanes = lax.broadcasted_iota(jnp.int32, (128, 128), 1)
    weights = 8.0 / (8.0 + jnp.abs(rows - lanes).astype(f32))
    stress = jnp.dot(weights, moments, precision=EXACT, preferred_element_type=f32)
    onehot = jnp.where(rows == cell_ref[...], 1.0, 0.0).T
    ts = jnp.dot(onehot, stress, precision=EXACT, preferred_element_type=f32)

    pick = jnp.concatenate([jnp.where(rows == nrow[c : c + 1, :], 1.0, 0.0).astype(bf16) for c in range(CAP)], 1)

    def gathered(ref, a, which):
        v = jnp.concatenate([ref[pl.ds(4 * c + a if which else 4 * a + c, 128, stride=16), :] for c in range(CAP)], 0)
        hi = v.astype(bf16)
        lo = (v - hi.astype(f32)).astype(bf16)
        return jnp.concatenate([hi, lo], 1)

    near = []
    for a in range(4):
        both = jnp.dot(pick, gathered(nraw, a, True), preferred_element_type=f32)
        near.append(both[:, :128] + both[:, 128:])
    for g in range(16):
        r = slice(8 * g, 8 * g + 8)
        pull = []
        for k in range(3):
            parts = [jnp.broadcast_to(ts[r, 3 * k + m : 3 * k + m + 1], (8, 128)) * seg[3 + m, r, :] for m in range(3)]
            pull.append(parts[0] + parts[1] + parts[2])
        line = [seg[6 + m, r, :] for m in range(3)]
        for a in range(3):
            p, q = (a + 1) % 3, (a + 2) % 3
            field = pull[p] * line[q] - pull[q] * line[p]
            out_ref[a, r, :] = seg[a, r, :] * near[3][r] - near[a][r] + field

    pltpu.make_async_remote_copy(
        src_ref=stage.at[pl.ds(1, PEERS - 1)], dst_ref=stage.at[pl.ds(1, PEERS - 1)], send_sem=out_send,
        recv_sem=out_recv.at[0], device_id=shifted(d, s, 1, 1), device_id_type=MESH).wait_send()
    pltpu.make_async_remote_copy(
        src_ref=stage.at[pl.ds(1, PEERS - 1), pl.ds(0, 12)], dst_ref=stage.at[pl.ds(1, PEERS - 1), pl.ds(0, 12)],
        send_sem=back_send, recv_sem=back_recv, device_id=shifted(d, s, 1, 1), device_id_type=MESH).wait()

    pick = jnp.concatenate([jnp.where(rows == send_ref[c : c + 1, :], 1.0, 0.0).astype(bf16) for c in range(CAP)], 1)
    for a in range(3):
        both = jnp.dot(pick, gathered(back, a, False), preferred_element_type=f32)
        out_ref[a] += both[:, :128] + both[:, 128:]


def on_device(segments, send_tiles, pair_local, pair_remote, pair_count, tile_cell):
    vm = pl.BlockSpec(memory_space=pltpu.VMEM)
    sm = pl.BlockSpec(memory_space=pltpu.SMEM)
    dma = pltpu.SemaphoreType.DMA
    slots = send_tiles[0].T
    forces = pl.pallas_call(
        exchange,
        out_shape=jax.ShapeDtypeStruct((3, 128, 128), f32),
        in_specs=[sm, pl.BlockSpec(memory_space=pl.ANY), vm, vm, vm, sm, vm],
        out_specs=vm,
        scratch_shapes=[
            pltpu.VMEM((9, 128, 128), f32),
            pltpu.VMEM((128, 9, 128), f32),
            pltpu.VMEM((PEERS, 36, 128), f32),
            pltpu.VMEM((PEERS * 40, 128), f32),
            pltpu.VMEM((PEERS * 16, 128), f32),
            pltpu.VMEM((PEERS * 16, 128), f32),
            pltpu.VMEM((129, 128, 128), bf16),
            pltpu.VMEM((129, 384, 128), f32),
            pltpu.VMEM((8 * K, 128), f32),
            pltpu.VMEM((GROUP // 2, 8 * FROWS, 128), f32),
            pltpu.VMEM((GROUP // 2, 256, 128), f32),
            pltpu.VMEM((16, 128), f32),
            pltpu.VMEM((8, 16, 128), f32),
            pltpu.VMEM((16, 16, 128), f32),
            pltpu.VMEM((8, 128), jnp.int32),
            pltpu.SMEM((8, 128), jnp.int32),
            dma(()),
            dma(()),
            dma((PEERS // GROUP,)),
            dma(()),
            dma(()),
            dma((4,)),
            dma(()),
            pltpu.SemaphoreType.REGULAR,
        ],
        compiler_params=pltpu.CompilerParams(
            collective_id=0, has_side_effects=True, vmem_limit_bytes=58 << 20
        ),
    )(
        slots,
        segments.transpose(1, 0, 2),
        slots,
        pair_local,
        pair_remote,
        pair_count,
        tile_cell.reshape(1, -1),
    )
    return forces.transpose(1, 0, 2)


def solution(mesh):
    in_specs = (
        P(("dom", "sub"), None, None),
        P(("dom", "sub"), None, None),
        P(("dom", "sub"), None),
        P(("dom", "sub"), None),
        P(("dom", "sub")),
        P(("dom", "sub")),
    )
    out_specs = P(("dom", "sub"), None, None)
    return jax.shard_map(
        on_device, mesh=mesh, in_specs=in_specs, out_specs=out_specs, check_vma=False
    )
```

time: 90.1 us -> 56.8 us (0.63)
  Pallas kernels: 77 us -> 54.3 us
  local copies, waits for them, and re-layouts: 8.72 us -> 1.62 us
  other arithmetic: 2.55 us -> 0 us
    pallas_call x2 -> x1, Pallas kernels: 77 us -> 54.3 us  [on_device(): pl.pallas_call(exchange, out_shape=jax.ShapeDtypeStruct((3, 128, 128), f3...]
    unnamed x22 -> x1, local copies, waits for them, and re-layouts: 4.66 us -> 1.62 us
    reshape x5 -> x0, local copies, waits for them, and re-layouts: 1.4 us -> none  [the longest x1 0.65 us: on_device(): send_flat = send_tiles.reshape(-1)]
    slice x2 -> x0, local copies, waits for them, and re-layouts: 1.12 us -> none  [the longest x1 1.11 us: local_moments(): segments[:, 3:6, None, :] * segments[:, None, 6:9, :]]
where the time goes in v2:
time: 56.8 us; the launch traced here: 56.5 us
  Pallas kernels  54.3 us (96%)
  local copies, waits for them, and re-layouts  1.62 us (3%)
  between operations  0.66 us (1%)
    pallas_call x1, Pallas kernels, on_device(): pl.pallas_call(exchange, out_shape=jax.ShapeDtypeStruct((3, 128, 128), f3...  54.3 us
    unnamed x1, local copies, waits for them, and re-layouts  1.62 us

profile of v2, /device:TPU:1, one launch (start us, length us, event | category | flops | bytes accessed | tf_op | source)
XLA Modules:
  0.0 56.5 jit_solution(13101737526626020653)
XLA Ops:
  0.7 54.3 %shard_map.64 = f32[3,128,128]{2,1,0:T(8,128)} custom-call(s32[4,128]{1,0:T(4,128)} %bitcast.8, f32[9,128,128]{2,1,0:T(8,128)} %bitcast.7, s32[4,128]{1,0:T(4,128)} %bitcast.9, s32[1,512]{1,0:T(1,128)} %local_ref.1, s32[1,512]{1,0:T(1,128)} %remote_ref.1, s32[1]{0:T(128)S(6)} %copy.8.count_ref, s32[1,128]{1,0:T(1,128)} %bitcast.10), custom_call_target="tpu_custom_call" | custom-call | tf_op jit(solution)/shard_map/pallas_call | solution.py:364
  54.9 1.6 %copy.9 = f32[128,3,128]{2,0,1:T(8,128)} copy(f32[128,3,128]{2,0,1:T(8,128)} %bitcast.6) | data formatting | bytes 393216

commit v3 on v2

--- a/solution.py
+++ b/solution.py
@@ -151,23 +151,27 @@
     return far, near_parts
 
 
+FIRST = 23
+
+
 def shifted(d, s, j, sign):
     k = (j * 37) & 127
-    dx, dz, dy = k >> 5, (k >> 3) & 3, (k >> 1) & 3
+    dx, dz, dy, dc = k >> 5, (k >> 3) & 3, (k >> 1) & 3, k & 1
     if sign < 0:
         dx, dz, dy = 4 - dx, 4 - dz, 4 - dy
     x = ((d >> 2) + dx) & 3
     z = ((d & 3) + dz) & 3
     y = ((s >> 1) + dy) & 3
-    c = ((s & 1) + (k & 1)) & 1
+    c = ((s & 1) + dc) & 1
     return x * 4 + z, y * 2 + c
 
 
 def exchange(
-    send_smem, seg_hbm, send_ref, local_ref, remote_ref, count_ref, cell_ref,
+    seg_hbm, send_hbm, local_hbm, remote_hbm, count_hbm, cell_hbm,
     out_ref,
+    send_smem, send_ref, local_ref, remote_ref, count_ref, cell_ref,
     seg, tiles, stage, recv, back, nraw, nft, spread, nscr, scr, part, mom, mom_a, mom_b, nrow, near_smem,
-    seg_sem, out_send, out_recv, back_send, back_recv, mom_sem, row_sem, stage_sem,
+    seg_sem, out_send, out_recv, back_send, back_recv, mom_sem, row_sem, arg_sem, stage_sem,
 ):
     d = lax.axis_index("dom")
     s = lax.axis_index("sub")
@@ -179,6 +183,61 @@
         pl.semaphore_signal(barrier, inc=1, device_id=((d + k) & 15, s), device_id_type=MESH)
     load = pltpu.make_async_copy(seg_hbm, seg, seg_sem)
     load.start()
+    moves = [
+        (send_hbm, send_smem), (local_hbm, local_ref), (remote_hbm, remote_ref),
+        (count_hbm, count_ref), (cell_hbm, cell_ref), (send_hbm, send_ref),
+    ]
+    moves = [pltpu.make_async_copy(a, b, arg_sem.at[i]) for i, (a, b) in enumerate(moves)]
+    for move in moves:
+        move.start()
+    load.wait()
+    for g in range(16):
+        for a in range(9):
+            tiles[8 * g : 8 * g + 8, a, :] = seg[a, 8 * g : 8 * g + 8, :]
+    for move in moves:
+        move.wait()
+
+    def gather(j):
+        td, ts = shifted(d, s, j, 1)
+        there = td * 8 + ts
+        for c in range(CAP):
+            stage[j, 9 * c : 9 * c + 9, :] = tiles[send_smem[c, there]]
+        return td, ts
+
+    def send(j, carry):
+        partner = gather(j)
+        pltpu.make_async_remote_copy(
+            src_ref=stage.at[j], dst_ref=recv.at[pl.ds(pl.multiple_of(j * 40, 8), 36)],
+            send_sem=out_send, recv_sem=out_recv.at[j // GROUP],
+            device_id=partner, device_id_type=MESH).start()
+        return carry
+
+    pl.semaphore_wait(barrier, 22)
+    for k in range(1, 8):
+        pl.semaphore_signal(stage_sem, inc=1, device_id=(d, (s + k) & 7), device_id_type=MESH)
+    pl.semaphore_wait(stage_sem, 7)
+    lax.fori_loop(1, FIRST, send, 0)
+
+    lane = lax.broadcasted_iota(jnp.int32, (128, 128), 1)
+    cells = lax.broadcasted_iota(jnp.int32, (128, 128), 0)
+    onehot = jnp.where(cells == cell_ref[...], 1.0, 0.0)
+    outer = jnp.zeros((128, 128), f32)
+    for a in range(3):
+        for b in range(3):
+            total = jnp.sum(seg[3 + a] * seg[6 + b], axis=1, keepdims=True)
+            outer = jnp.where(lane == 3 * a + b, total, outer)
+    sums = jnp.dot(onehot, outer, precision=EXACT, preferred_element_type=f32).T
+    last = jnp.concatenate([jnp.zeros((1, NCELL), f32), sums[8:9, :NCELL]], 1)
+    mom[...] = sums[0:8] + jnp.concatenate([last, jnp.zeros((7, 128), f32)], 0)
+    mom_a[0] = mom[...]
+    for k in range(1, 8):
+        pltpu.make_async_remote_copy(
+            src_ref=mom, dst_ref=mom_a.at[k], send_sem=mom_sem.at[0], recv_sem=mom_sem.at[1],
+            device_id=(d, (s + k) & 7), device_id_type=MESH).start()
+
+    lax.fori_loop(FIRST, PEERS, send, 0)
+    gather(0)
+    recv[0:36, :] = stage[0]
 
     remote = remote_ref[...]
     slot = (remote & 3) * 128 + (remote >> 2)
@@ -193,51 +252,6 @@
     nrow[4:8, :] = jnp.zeros((4, 128), jnp.int32)
     to_smem = pltpu.make_async_copy(nrow, near_smem, row_sem)
     to_smem.start()
-
-    load.wait()
-    for g in range(16):
-        for a in range(9):
-            tiles[8 * g : 8 * g + 8, a, :] = seg[a, 8 * g : 8 * g + 8, :]
-
-    def gather(j, carry):
-        td, ts = shifted(d, s, j, 1)
-        there = td * 8 + ts
-        for c in range(CAP):
-            stage[j, 9 * c : 9 * c + 9, :] = tiles[send_smem[c, there]]
-        return carry
-
-    lax.fori_loop(0, PEERS, gather, 0)
-    recv[0:36, :] = stage[0]
-
-    lane = lax.broadcasted_iota(jnp.int32, (128, 128), 1)
-    cells = lax.broadcasted_iota(jnp.int32, (128, 128), 0)
-    onehot = jnp.where(cells == cell_ref[...], 1.0, 0.0)
-    outer = jnp.zeros((128, 128), f32)
-    for a in range(3):
-        for b in range(3):
-            total = jnp.sum(seg[3 + a] * seg[6 + b], axis=1, keepdims=True)
-            outer = jnp.where(lane == 3 * a + b, total, outer)
-    mom[...] = jnp.dot(onehot, outer, precision=EXACT, preferred_element_type=f32).T[0:16]
-    mom_a[0] = mom[...]
-
-    pl.semaphore_wait(barrier, 22)
-    for k in range(1, 8):
-        pl.semaphore_signal(stage_sem, inc=1, device_id=(d, (s + k) & 7), device_id_type=MESH)
-    pl.semaphore_wait(stage_sem, 7)
-
-    for k in range(1, 8):
-        pltpu.make_async_remote_copy(
-            src_ref=mom, dst_ref=mom_a.at[k], send_sem=mom_sem.at[0], recv_sem=mom_sem.at[1],
-            device_id=(d, (s + k) & 7), device_id_type=MESH).start()
-
-    def send(j, carry):
-        pltpu.make_async_remote_copy(
-            src_ref=stage.at[j], dst_ref=recv.at[pl.ds(pl.multiple_of(j * 40, 8), 36)],
-            send_sem=out_send, recv_sem=out_recv.at[j // GROUP],
-            device_id=shifted(d, s, j, 1), device_id_type=MESH).start()
-        return carry
-
-    lax.fori_loop(1, PEERS, send, 0)
     prepare_near(seg, nft, spread, nscr)
 
     a_all = pltpu.make_async_remote_copy(
@@ -308,10 +322,12 @@
         src_ref=mom_b.at[pl.ds(1, 15)], dst_ref=mom_b.at[pl.ds(1, 15)], send_sem=mom_sem.at[2], recv_sem=mom_sem.at[3],
         device_id=((d + 1) & 15, s), device_id_type=MESH)
     b_all.wait()
-    sums = jnp.sum(mom_b[...], 0)
+    packed = jnp.sum(mom_b[...], 0)
+    sums = [packed[r : r + 1, :NCELL] for r in range(8)] + [packed[0:1, NCELL:]]
     scale = 0.5 / math.sqrt(PEERS * 128 * 128)
-    sym = [(sums[3 * a + b : 3 * a + b + 1] + sums[3 * b + a : 3 * b + a + 1]) * scale for a in range(3) for b in range(3)]
-    moments = jnp.concatenate(sym + [jnp.zeros((128 - 9, 128), f32)], 0).T
+    sym = [(sums[3 * a + b] + sums[3 * b + a]) * scale for a in range(3) for b in range(3)]
+    sym = jnp.concatenate(sym + [jnp.zeros((128 - 9, NCELL), f32)], 0)
+    moments = jnp.concatenate([sym, jnp.zeros((128, 128 - NCELL), f32)], 1).T
     rows = lax.broadcasted_iota(jnp.int32, (128, 128), 0)
     lanes = lax.broadcasted_iota(jnp.int32, (128, 128), 1)
     weights = 8.0 / (8.0 + jnp.abs(rows - lanes).astype(f32))
@@ -358,15 +374,20 @@
 
 def on_device(segments, send_tiles, pair_local, pair_remote, pair_count, tile_cell):
     vm = pl.BlockSpec(memory_space=pltpu.VMEM)
-    sm = pl.BlockSpec(memory_space=pltpu.SMEM)
     dma = pltpu.SemaphoreType.DMA
     slots = send_tiles[0].T
     forces = pl.pallas_call(
         exchange,
         out_shape=jax.ShapeDtypeStruct((3, 128, 128), f32),
-        in_specs=[sm, pl.BlockSpec(memory_space=pl.ANY), vm, vm, vm, sm, vm],
+        in_specs=[pl.BlockSpec(memory_space=pl.ANY)] * 6,
         out_specs=vm,
         scratch_shapes=[
+            pltpu.SMEM((CAP, 128), jnp.int32),
+            pltpu.VMEM((CAP, 128), jnp.int32),
+            pltpu.VMEM((1, 512), jnp.int32),
+            pltpu.VMEM((1, 512), jnp.int32),
+            pltpu.SMEM((1,), jnp.int32),
+            pltpu.VMEM((1, 128), jnp.int32),
             pltpu.VMEM((9, 128, 128), f32),
             pltpu.VMEM((128, 9, 128), f32),
             pltpu.VMEM((PEERS, 36, 128), f32),
@@ -378,9 +399,9 @@
             pltpu.VMEM((8 * K, 128), f32),
             pltpu.VMEM((GROUP // 2, 8 * FROWS, 128), f32),
             pltpu.VMEM((GROUP // 2, 256, 128), f32),
-            pltpu.VMEM((16, 128), f32),
-            pltpu.VMEM((8, 16, 128), f32),
-            pltpu.VMEM((16, 16, 128), f32),
+            pltpu.VMEM((8, 128), f32),
+            pltpu.VMEM((8, 8, 128), f32),
+            pltpu.VMEM((16, 8, 128), f32),
             pltpu.VMEM((8, 128), jnp.int32),
             pltpu.SMEM((8, 128), jnp.int32),
             dma(()),
@@ -390,13 +411,13 @@
             dma(()),
             dma((4,)),
             dma(()),
+            dma((6,)),
             pltpu.SemaphoreType.REGULAR,
         ],
         compiler_params=pltpu.CompilerParams(
             collective_id=0, has_side_effects=True, vmem_limit_bytes=58 << 20
         ),
     )(
-        slots,
         segments.transpose(1, 0, 2),
         slots,
         pair_local,

time: 56.8 us -> 55 us (0.968)
  Pallas kernels: 54.3 us -> 52.6 us
    pallas_call x1, Pallas kernels: 54.3 us -> 52.6 us  [on_device(): pl.pallas_call(exchange, out_shape=jax.ShapeDtypeStruct((3, 128, 128), f3...]
where the time goes in v3:
time: 55 us; the launch traced here: 54.8 us
  Pallas kernels  52.6 us (96%)
  local copies, waits for them, and re-layouts  1.62 us (3%)
  between operations  0.66 us (1%)
    pallas_call x1, Pallas kernels, on_device(): pl.pallas_call(exchange, out_shape=jax.ShapeDtypeStruct((3, 128, 128), f3...  52.6 us
    unnamed x1, local copies, waits for them, and re-layouts  1.62 us

profile of v3, /device:TPU:1, one launch (start us, length us, event | category | flops | bytes accessed | tf_op | source)
XLA Modules:
  0.0 54.8 jit_solution(7910307745708728610)
XLA Ops:
  0.7 52.6 %shard_map.64 = f32[3,128,128]{2,1,0:T(8,128)} custom-call(f32[9,128,128]{2,1,0:T(8,128)} %bitcast.7, s32[4,128]{1,0:T(4,128)} %bitcast.8, s32[1,512]{1,0:T(1,128)} %local_hbm.1, s32[1,512]{1,0:T(1,128)} %remote_hbm.1, s32[1]{0:T(128)S(6)} %copy.8.count_hbm, s32[1,128]{1,0:T(1,128)} %bitcast.9), custom_call_target="tpu_custom_call" | custom-call | tf_op jit(solution)/shard_map/pallas_call | solution.py:379
  53.2 1.6 %copy.9 = f32[128,3,128]{2,0,1:T(8,128)} copy(f32[128,3,128]{2,0,1:T(8,128)} %bitcast.6) | data formatting | bytes 393216

commit v4 on v3

--- a/solution.py
+++ b/solution.py
@@ -155,7 +155,7 @@
 
 
 def shifted(d, s, j, sign):
-    k = (j * 37) & 127
+    k = (j * 101) & 127
     dx, dz, dy, dc = k >> 5, (k >> 3) & 3, (k >> 1) & 3, k & 1
     if sign < 0:
         dx, dz, dy = 4 - dx, 4 - dz, 4 - dy

time: 55 us -> 54.8 us (level)
  no operation moved by 1% of the time
where the time goes in v4:
time: 54.8 us; the launch traced here: 54.6 us
  Pallas kernels  52.4 us (96%)
  local copies, waits for them, and re-layouts  1.62 us (3%)
  between operations  0.66 us (1%)
    pallas_call x1, Pallas kernels, on_device(): pl.pallas_call(exchange, out_shape=jax.ShapeDtypeStruct((3, 128, 128), f3...  52.4 us
    unnamed x1, local copies, waits for them, and re-layouts  1.62 us

profile of v4, /device:TPU:1, one launch (start us, length us, event | category | flops | bytes accessed | tf_op | source)
XLA Modules:
  0.0 54.6 jit_solution(5993232836062122108)
XLA Ops:
  0.7 52.4 %shard_map.64 = f32[3,128,128]{2,1,0:T(8,128)} custom-call(f32[9,128,128]{2,1,0:T(8,128)} %bitcast.7, s32[4,128]{1,0:T(4,128)} %bitcast.8, s32[1,512]{1,0:T(1,128)} %local_hbm.1, s32[1,512]{1,0:T(1,128)} %remote_hbm.1, s32[1]{0:T(128)S(6)} %copy.8.count_hbm, s32[1,128]{1,0:T(1,128)} %bitcast.9), custom_call_target="tpu_custom_call" | custom-call | tf_op jit(solution)/shard_map/pallas_call | solution.py:379
  53.0 1.6 %copy.9 = f32[128,3,128]{2,0,1:T(8,128)} copy(f32[128,3,128]{2,0,1:T(8,128)} %bitcast.6) | data formatting | bytes 393216
